TPU v7x, 128 devices: a whole 4x4x4 slice. The times are simulated.
128 devices in a mesh: seq: 16 (over z, y), exp: 8 (over x, core).
Axes of the slice: x: 4, y: 4, z: 4, core: 2. Of those that a mesh axis runs over, the one named last changes fastest.
Arguments:
- tokens: bfloat16 [8192, 2048], P('seq', 'exp'), may hold values from -6 to 6
- grad_out: bfloat16 [8192, 2048], P('seq', 'exp'), may hold values from -6 to 6
- chosen: int32 [16, 512], replicated, may hold values from 0 to 8191, as said below
- scores: float32 [16, 512], P('seq'), may hold values from 0.2 to 2
- gate_weight: bfloat16 [16, 2048, 8192], P('seq', None, 'exp'), may hold values from -0.125 to 0.125
- up_weight: bfloat16 [16, 2048, 8192], P('seq', None, 'exp'), may hold values from -0.125 to 0.125
- down_weight: bfloat16 [16, 8192, 2048], P('seq', 'exp'), may hold values from -0.0625 to 0.0625
Outputs:
- grad_tokens: bfloat16 [8192, 2048], P('seq', 'exp')
- grad_scores: float32 [16, 512], P('seq')
- grad_gate: bfloat16 [16, 2048, 8192], P('seq', None, 'exp')
- grad_up: bfloat16 [16, 2048, 8192], P('seq', None, 'exp')
- grad_down: bfloat16 [16, 8192, 2048], P('seq', 'exp')
Inputs may be any that keep to these rules, and one draw needn't show every extreme that they name: `chosen`: each row holds 512 distinct token indices in ascending order. For every expert and every owner o (tokens o * 512 to (o + 1) * 512 - 1) at most 64 of its indices lie with o, and exactly 64 for some owner of every expert.
All inputs are finite; a program needn't handle non-finite values.
Results may differ from a plain program's by a relative error of at most 0.007.
Values may be sent and summed in bfloat16 or wider, within the bound.
A program may use at most 128 MiB of HBM per device.

v0:
```python
import jax
import jax.numpy as jnp
from jax import lax
from jax.sharding import PartitionSpec as P


def send_lists(chosen, owner_id, tok_dev, most):
    width = chosen.shape[1]
    lower = owner_id * tok_dev
    begins = jnp.sum(chosen < lower, axis=1)
    ends = jnp.sum(chosen < lower + tok_dev, axis=1)
    slot_ids = jnp.arange(most, dtype=jnp.int32)
    picks = jnp.minimum(begins[:, None] + slot_ids[None, :], width - 1)
    usable = slot_ids[None, :] < (ends - begins)[:, None]
    local = jnp.take_along_axis(chosen, picks, axis=1) - lower
    local = jnp.where(usable, local, 0)
    return (local, usable)


def receive_lists(picked, owners, tok_dev, most):
    width = picked.shape[0]
    bounds = jnp.arange(owners + 1, dtype=jnp.int32) * tok_dev
    begins_all = jnp.sum(picked[None, :] < bounds[:, None], axis=1)
    begins = begins_all[:-1]
    counts = begins_all[1:] - begins
    source = picked // tok_dev
    onehot = source[:, None] == jnp.arange(owners, dtype=jnp.int32)[None, :]
    first = jnp.sum(jnp.where(onehot, begins[None, :], 0), axis=1)
    flat = source * most + jnp.arange(width, dtype=jnp.int32) - first
    slot_ids = jnp.arange(most, dtype=jnp.int32)
    picks = jnp.minimum(begins[:, None] + slot_ids[None, :], width - 1)
    usable = slot_ids[None, :] < counts[:, None]
    return (flat, picks, usable)


def shards(tokens, grad_out, chosen, scores, gate_weight, up_weight, down_weight):
    owner_id = lax.axis_index("seq")
    owners = lax.axis_size("seq")
    tok_dev = tokens.shape[0]
    width = chosen.shape[1]
    most = 2 * width // owners
    local, sendable = send_lists(chosen, owner_id, tok_dev, most)
    mask_send = sendable[:, :, None]
    wide_tokens, wide_grads = (
        lax.all_gather(tokens, "exp", axis=1, tiled=True),
        lax.all_gather(grad_out, "exp", axis=1, tiled=True),
    )
    out_rows = jnp.where(mask_send, wide_tokens[local], 0)
    out_grads = jnp.where(mask_send, wide_grads[local], 0)
    recv_rows, recv_grads = (
        lax.all_to_all(out_rows, "seq", split_axis=0, concat_axis=0, tiled=True),
        lax.all_to_all(out_grads, "seq", split_axis=0, concat_axis=0, tiled=True),
    )
    picked = lax.dynamic_index_in_dim(chosen, owner_id, 0, keepdims=False)
    flat, picks, usable = receive_lists(picked, owners, tok_dev, most)
    full_width = recv_rows.shape[2]
    rows = recv_rows.reshape(owners * most, full_width)[flat]
    grads = recv_grads.reshape(owners * most, full_width)[flat]
    gains = scores[0]
    gate_mat = gate_weight[0]
    up_mat = up_weight[0]
    down_mat = down_weight[0]
    gate_pre = jnp.dot(rows, gate_mat, preferred_element_type=jnp.float32)
    up_pre = jnp.dot(rows, up_mat, preferred_element_type=jnp.float32)
    sigma = jax.nn.sigmoid(gate_pre)
    silu_gate = gate_pre * sigma
    hidden = (silu_gate * up_pre).astype(jnp.bfloat16)
    back_hidden = lax.dot_general(
        grads, down_mat, (((1,), (1,)), ((), ())), preferred_element_type=jnp.float32
    )
    score_part = jnp.sum(hidden.astype(jnp.float32) * back_hidden, axis=1)
    grad_scores = lax.psum(score_part, "exp")
    scaled = (gains[:, None] * grads.astype(jnp.float32)).astype(jnp.bfloat16)
    grad_down = lax.dot_general(
        hidden, scaled, (((0,), (0,)), ((), ())), preferred_element_type=jnp.float32
    ).astype(jnp.bfloat16)
    hidden_grad = gains[:, None] * back_hidden
    grad_gate_pre = (hidden_grad * up_pre * sigma * (1.0 + gate_pre * (1.0 - sigma))).astype(
        jnp.bfloat16
    )
    grad_up_pre = (hidden_grad * silu_gate).astype(jnp.bfloat16)
    partial_value = lax.dot_general(
        grad_gate_pre, gate_mat, (((1,), (1,)), ((), ())), preferred_element_type=jnp.float32
    )
    partial_value = partial_value + lax.dot_general(
        grad_up_pre, up_mat, (((1,), (1,)), ((), ())), preferred_element_type=jnp.float32
    )
    summed = lax.psum_scatter(partial_value, "exp", scatter_dimension=1, tiled=True).astype(
        jnp.bfloat16
    )
    outgoing = jnp.where(usable[:, :, None], summed[picks], 0)
    returned = lax.all_to_all(outgoing, "seq", split_axis=0, concat_axis=0, tiled=True)
    grad_gate = lax.dot_general(
        rows, grad_gate_pre, (((0,), (0,)), ((), ())), preferred_element_type=jnp.float32
    ).astype(jnp.bfloat16)
    grad_up = lax.dot_general(
        rows, grad_up_pre, (((0,), (0,)), ((), ())), preferred_element_type=jnp.float32
    ).astype(jnp.bfloat16)
    slice_width = returned.shape[2]
    contrib = jnp.where(mask_send, returned.astype(jnp.float32), 0.0)
    total = jnp.zeros((tok_dev, slice_width), jnp.float32)
    total = total.at[local.reshape(-1)].add(contrib.reshape(-1, slice_width))
    return (
        total.astype(jnp.bfloat16),
        grad_scores[None, :],
        grad_gate[None],
        grad_up[None],
        grad_down[None],
    )


def solution(mesh):
    in_specs = (
        P("seq", "exp"),
        P("seq", "exp"),
        P(),
        P("seq", None),
        P("seq", None, "exp"),
        P("seq", None, "exp"),
        P("seq", "exp", None),
    )
    out_specs = (
        P("seq", "exp"),
        P("seq", None),
        P("seq", None, "exp"),
        P("seq", None, "exp"),
        P("seq", "exp", None),
    )
    return jax.shard_map(shards, mesh=mesh, in_specs=in_specs, out_specs=out_specs, check_vma=False)
```

profile of v0, /device:TPU:0, one launch (start us, length us, event | category | flops | bytes accessed | tf_op | source)
XLA Modules:
  0.0 307.3 jit_solution(8374738123609552750)
XLA Ops:
  7.2 0.7 all-gather.3.cloned.1.call-update
  8.0 0.7 all-gather.5.cloned.1.call-update
  8.7 0.9 convert_reduce_fusion.1
  9.7 8.6 %gather_fusion.5 = s32[1024]{0:T(1024)S(1)} fusion(s32[16,512]{1,0:T(8,128)S(1)} %copy-done, s32[1024]{0:T(1024)S(1)} %reshape.486), kind=kCustom, calls=%fused_computation.5 | custom fusion | bytes 16384 | tf_op jit(solution)/shard_map/jit(take_along_axis)/gather | solution.py:15
  18.6 20.8 %all-gather.3.cloned.1.call-done = bf16[512,2048]{1,0:T(8,128)(2,1)} async-done(((bf16[512,256]{1,0:T(8,128)(2,1)}), bf16[512,2048]{1,0:T(8,128)(2,1)}) %all-gather.3.cloned.1.call-update) | async-done | bytes 2097168 | tf_op jit(solution)/shard_map/all_gather | solution.py:46
  39.4 10.7 %gather_fusion = bf16[1024,2048]{1,0:T(8,128)(2,1)} fusion(bf16[512,2048]{1,0:T(8,128)(2,1)} %all-gather.3.cloned.1.call-done, s32[1024]{0:T(1024)S(1)} %broadcast_clamp_fusion.1), kind=kCustom, calls=%fused_computation | custom fusion | bytes 8392704 | tf_op jit(solution)/shard_map/gather | solution.py:49
  50.1 19.3 %all-gather.5.cloned.1.call-done = bf16[512,2048]{1,0:T(8,128)(2,1)} async-done(((bf16[512,256]{1,0:T(8,128)(2,1)}), bf16[512,2048]{1,0:T(8,128)(2,1)}) %all-gather.5.cloned.1.call-update) | async-done | bytes 2097168 | tf_op jit(solution)/shard_map/all_gather | solution.py:45
  69.3 10.7 %gather_fusion.2 = bf16[1024,2048]{1,0:T(8,128)(2,1)} fusion(bf16[512,2048]{1,0:T(8,128)(2,1)} %all-gather.5.cloned.1.call-done, s32[1024]{0:T(1024)S(1)} %broadcast_clamp_fusion.1), kind=kCustom, calls=%fused_computation.2 | custom fusion | bytes 8392704 | tf_op jit(solution)/shard_map/gather | solution.py:48
  80.0 5.1 %broadcast_select_fusion.1 = (bf16[16,64,2048]{2,1,0:T(8,128)(2,1)}, bf16[16,64,2048]{2,1,0:T(8,128)(2,1)S(1)}) fusion(bf16[16,64,2048]{2,1,0:T(8,128)(2,1)} %bitcast.67, pred[16,64]{1,0:T(8,128)(4,1)S(1)} %iota_compare_fusion.3, bf16[16,64,2048]{2,1,0:T(8,128)(2,1)} %bitcast.68), kind=kLoop, calls=%fused_computation.22 | loop fusion | flops 4194304 | bytes 16778240 | tf_op jit(solution)/shard_map/jit(_where)/select_n | solution.py:49
  85.1 58.1 %all_to_all.15 = bf16[16,64,2048]{2,1,0:T(8,128)(2,1)} all-to-all(bf16[16,64,2048]{2,1,0:T(8,128)(2,1)S(1)} %get-tuple-element.12), channel_id=1, replica_groups=mesh['seq'=16,'exp'=8] {'seq'}, dimensions={0} | all-to-all | bytes 8388608 | tf_op jit(solution)/shard_map/all_to_all | solution.py:51
  143.3 4.5 %all-to-all-start = ((bf16[16,64,2048]{2,1,0:T(8,128)(2,1)}), bf16[16,64,2048]{2,1,0:T(8,128)(2,1)}, u32[]{:S(2)}, u32[]{:S(2)}) async-start(bf16[16,64,2048]{2,1,0:T(8,128)(2,1)} %get-tuple-element.11), calls=%async_computation | async-start | bytes 8388608 | tf_op jit(solution)/shard_map/all_to_all | solution.py:52
  148.5 7.1 %gather_fusion.3 = bf16[512,2048]{1,0:T(8,128)(2,1)S(1)} fusion(bf16[1024,2048]{1,0:T(8,128)(2,1)} %bitcast.66, s32[1024]{0:T(1024)S(1)} %pad_clamp_fusion), kind=kCustom, calls=%fused_computation.3 | custom fusion | bytes 4196352 | tf_op jit(solution)/shard_map/gather | solution.py:57
  155.6 6.0 %fusion.6 = f32[512,1024]{1,0:T(8,128)} fusion(bf16[512,2048]{1,0:T(8,128)(2,1)S(1)} %gather_fusion.3, bf16[1,2048,1024]{2,1,0:T(8,128)(2,1)} %param.12), kind=kOutput, calls=%fused_computation.13 | convolution fusion | flops 2147483648 | bytes 8388608 | tf_op jit(solution)/shard_map/dot_general | solution.py:64
  161.6 3.7 %fusion.2 = f32[512,1024]{1,0:T(8,128)} fusion(bf16[512,2048]{1,0:T(8,128)(2,1)S(1)} %gather_fusion.3, bf16[1,2048,1024]{2,1,0:T(8,128)(2,1)S(1)} %copy-done.2), kind=kOutput, calls=%fused_computation.9 | convolution fusion | flops 2147483648 | bytes 8388608 | tf_op jit(solution)/shard_map/dot_general | solution.py:63
  165.3 43.5 %all-to-all-done = bf16[16,64,2048]{2,1,0:T(8,128)(2,1)} async-done(((bf16[16,64,2048]{2,1,0:T(8,128)(2,1)}), bf16[16,64,2048]{2,1,0:T(8,128)(2,1)}, u32[]{:S(2)}, u32[]{:S(2)}) %all-to-all-start) | async-done | bytes 4194336 | tf_op jit(solution)/shard_map/all_to_all | solution.py:52
  208.9 8.0 %gather_fusion.1 = bf16[512,2048]{1,0:T(8,128)(2,1)} fusion(bf16[1024,2048]{1,0:T(8,128)(2,1)} %bitcast.5, s32[1024]{0:T(1024)S(1)} %pad_clamp_fusion), kind=kCustom, calls=%fused_computation.1 | custom fusion | bytes 4196352 | tf_op jit(solution)/shard_map/gather | solution.py:58
  216.8 8.4 %multiply_reduce_fusion = (f32[512]{0:T(512)S(1)}, bf16[512,1024]{1,0:T(8,128)(2,1)}, bf16[512,1024]{1,0:T(8,128)(2,1)S(1)}, bf16[512,1024]{1,0:T(8,128)(2,1)S(1)}) fusion(f32[512,1024]{1,0:T(8,128)} %fusion.6, f32[512,1024]{1,0:T(8,128)} %fusion.2, f32[512]{0:T(512)S(1)} %bitcast.78, bf16[512,2048]{1,0:T(8,128)(2,1)} %gather_fusion.1, ...), kind=kOutput, calls=%fused_computation.25 | convolution fusion | flops 2157444608 | bytes 13635584 | tf_op jit(solution)/shard_map/dot_general | solution.py:68
  225.3 2.4 fusion
  227.7 0.5 copy-done.4
  228.2 4.4 %fusion.10 = f32[512,2048]{1,0:T(8,128)} fusion(f32[512,2048]{1,0:T(8,128)S(1)} %fusion, bf16[512,1024]{1,0:T(8,128)(2,1)S(1)} %get-tuple-element.10, bf16[1,2048,1024]{2,1,0:T(8,128)(2,1)S(1)} %copy-done.4), kind=kOutput, calls=%fused_computation.23 | convolution fusion | flops 2148532224 | bytes 13631488 | tf_op jit(solution)/shard_map/dot_general | solution.py:85
  233.2 13.3 %psum.7 = f32[1,512]{1,0:T(1,128)} all-reduce(f32[1,512]{1,0:T(1,128)S(1)} %bitcast.77), channel_id=1, replica_groups=mesh['seq'=16,'exp'=8] {'exp'}, use_global_device_ids=true, to_apply=%region_7.8 | all-reduce | flops 512 | bytes 4096 | tf_op jit(solution)/shard_map/psum | solution.py:72
  246.5 5.8 %convert_bitcast_fusion.2 = bf16[1,2048,1024]{2,1,0:T(8,128)(2,1)} fusion(bf16[512,2048]{1,0:T(8,128)(2,1)S(1)} %gather_fusion.3, bf16[512,1024]{1,0:T(8,128)(2,1)} %copy-done.6), kind=kOutput, calls=%fused_computation.20 | convolution fusion | flops 2149580800 | bytes 7340032 | tf_op jit(solution)/shard_map/dot_general | solution.py:93
  252.3 4.5 %convert_bitcast_fusion = bf16[1,1024,2048]{2,1,0:T(8,128)(2,1)} fusion(bf16[512,1024]{1,0:T(8,128)(2,1)S(1)} %copy-done.8, bf16[512,2048]{1,0:T(8,128)(2,1)S(1)} %copy-done.1, f32[512]{0:T(512)S(1)} %bitcast.79), kind=kOutput, calls=%fused_computation.17 | convolution fusion | flops 2152726528 | bytes 7342080 | tf_op jit(solution)/shard_map/dot_general | solution.py:74
  256.8 12.7 %reduce-scatter.2.cloned.1.call-done = f32[512,256]{1,0:T(8,128)} async-done(((f32[512,2048]{1,0:T(8,128)}), f32[512,256]{1,0:T(8,128)}) %reduce-scatter.2.cloned.1.call-update) | async-done | bytes 524304 | tf_op jit(solution)/shard_map/reduce_scatter | solution.py:88
  269.6 1.1 convert_element_type.55
  270.6 3.9 %gather_fusion.4 = bf16[1024,256]{1,0:T(8,128)(2,1)S(1)} fusion(bf16[512,256]{1,0:T(8,128)(2,1)S(1)} %convert_element_type.55, s32[1024]{0:T(1024)S(1)} %broadcast_clamp_fusion), kind=kCustom, calls=%fused_computation.4 | custom fusion | bytes 1052672 | tf_op jit(solution)/shard_map/gather | solution.py:91
  274.6 1.0 broadcast_select_fusion.2
  275.6 6.9 %all-to-all-start.2 = ((bf16[16,64,256]{2,1,0:T(8,128)(2,1)}), bf16[16,64,256]{2,1,0:T(8,128)(2,1)S(1)}, u32[]{:S(2)}, u32[]{:S(2)}) async-start(bf16[16,64,256]{2,1,0:T(8,128)(2,1)} %broadcast_select_fusion.2), calls=%async_computation.3 | async-start | bytes 1048576 | tf_op jit(solution)/shard_map/all_to_all | solution.py:92
  282.5 5.6 %convert_bitcast_fusion.1 = bf16[1,2048,1024]{2,1,0:T(8,128)(2,1)} fusion(bf16[512,2048]{1,0:T(8,128)(2,1)S(1)} %gather_fusion.3, bf16[512,1024]{1,0:T(8,128)(2,1)} %copy-done.7), kind=kOutput, calls=%fused_computation.19 | convolution fusion | flops 2149580800 | bytes 7340032 | tf_op jit(solution)/shard_map/dot_general | solution.py:96
  288.1 4.5 %all-to-all-done.2 = bf16[16,64,256]{2,1,0:T(8,128)(2,1)S(1)} async-done(((bf16[16,64,256]{2,1,0:T(8,128)(2,1)}), bf16[16,64,256]{2,1,0:T(8,128)(2,1)S(1)}, u32[]{:S(2)}, u32[]{:S(2)}) %all-to-all-start.2) | async-done | bytes 524320 | tf_op jit(solution)/shard_map/all_to_all | solution.py:92
  292.8 7.2 %scatter_custom_fusion = f32[512,256]{1,0:T(8,128)S(1)} fusion(s32[1024]{0:T(1024)S(1)} %bitcast.76, f32[1024,256]{1,0:T(8,128)S(1)} %bitcast.70, f32[]{:T(128)} %constant.19.clone.1), kind=kCustom, calls=%fused_computation.33 | custom fusion | flops 262144 | bytes 524292 | tf_op jit(solution)/shard_map/scatter-add | solution.py:102
  300.0 0.7 convert_element_type.57
  (48 shorter events, 2.0 us)
Async XLA Ops:
  7.2 2.5 copy-start
  7.2 32.2 %all-gather.3.cloned.1.call-start = ((), (), s32[]{:S(2)}) async-start(), calls=%async_computation.4 | async-start | bytes 2359296 | tf_op jit(solution)/shard_map/all_gather | solution.py:46
  7.9 61.4 %all-gather.5.cloned.1.call-start = ((), (), s32[]{:S(2)}) async-start(), calls=%async_computation.5 | async-start | bytes 2359296 | tf_op jit(solution)/shard_map/all_gather | solution.py:45
  143.3 65.6 %all-to-all-start = ((bf16[16,64,2048]{2,1,0:T(8,128)(2,1)}), bf16[16,64,2048]{2,1,0:T(8,128)(2,1)}, u32[]{:S(2)}, u32[]{:S(2)}) async-start(bf16[16,64,2048]{2,1,0:T(8,128)(2,1)} %get-tuple-element.11), calls=%async_computation | async-start | bytes 8388608 | tf_op jit(solution)/shard_map/all_to_all | solution.py:52
  147.8 121.7 %reduce-scatter.2.cloned.1.call-start = ((), (), s32[]{:S(2)}) async-start(), calls=%async_computation.6 | async-start | bytes 4718592 | tf_op jit(solution)/shard_map/reduce_scatter | solution.py:88
  155.6 6.0 %copy-start.2 = (bf16[1,2048,1024]{2,1,0:T(8,128)(2,1)S(1)}, bf16[1,2048,1024]{2,1,0:T(8,128)(2,1)}, u32[]{:S(2)}) copy-start(bf16[1,2048,1024]{2,1,0:T(8,128)(2,1)} %param.11) | copy-start | bytes 12582916
  208.9 8.0 %copy-start.5 = (f32[1,512]{1,0:T(1,128)S(1)}, f32[1,512]{1,0:T(1,128)}, u32[]{:S(2)}) copy-start(f32[1,512]{1,0:T(1,128)} %param.10) | copy-start | bytes 6148
  216.8 8.4 %copy-start.3 = (bf16[1,2048,1024]{2,1,0:T(8,128)(2,1)S(1)}, bf16[1,2048,1024]{2,1,0:T(8,128)(2,1)}, u32[]{:S(2)}) copy-start(bf16[1,2048,1024]{2,1,0:T(8,128)(2,1)} %param.11) | copy-start | bytes 12582916
  225.3 2.4 copy-start.6
  225.3 2.4 copy-start.7
  225.3 2.9 copy-start.4
  246.5 5.8 %copy-start.1 = (bf16[512,2048]{1,0:T(8,128)(2,1)S(1)}, bf16[512,2048]{1,0:T(8,128)(2,1)}, u32[]{:S(2)}) copy-start(bf16[512,2048]{1,0:T(8,128)(2,1)} %gather_fusion.1) | copy-start | bytes 6291460
  246.5 5.8 %copy-start.8 = (bf16[512,1024]{1,0:T(8,128)(2,1)S(1)}, bf16[512,1024]{1,0:T(8,128)(2,1)}, u32[]{:S(2)}) copy-start(bf16[512,1024]{1,0:T(8,128)(2,1)} %get-tuple-element.8) | copy-start | bytes 3145732
  275.6 17.0 %all-to-all-start.2 = ((bf16[16,64,256]{2,1,0:T(8,128)(2,1)}), bf16[16,64,256]{2,1,0:T(8,128)(2,1)S(1)}, u32[]{:S(2)}, u32[]{:S(2)}) async-start(bf16[16,64,256]{2,1,0:T(8,128)(2,1)} %broadcast_select_fusion.2), calls=%async_computation.3 | async-start | bytes 1048576 | tf_op jit(solution)/shard_map/all_to_all | solution.py:92
Sparse Core Ops, SparseCore 0:
  9.7 29.6 all-gather.2
  41.1 28.2 all-gather.4
  232.8 36.7 reduce-scatter.1
where the time goes:
time: 308 us; the launch traced here: 307 us
  waiting for transfers between devices  102 us (33%)
  blocking collectives  71.4 us (23%)
  local copies, waits for them, and re-layouts  50.2 us (16%)
  matrix products  40.8 us (13%)
  other arithmetic  17 us (6%)
  between operations  13.9 us (5%)
  starting transfers between devices  11.7 us (4%)
    all_to_all x1, blocking collectives, shards(): lax.all_to_all(out_rows, 'seq', split_axis=0, concat_axis=0, tiled=True)  58.1 us
    all_to_all x1, waiting for transfers between devices, shards(): lax.all_to_all(out_grads, 'seq', split_axis=0, concat_axis=0, tiled=True)  43.5 us
    all_gather x1, waiting for transfers between devices, shards(): lax.all_gather(grad_out, 'exp', axis=1, tiled=True)  20.8 us
    all_gather x1, waiting for transfers between devices, shards(): lax.all_gather(tokens, 'exp', axis=1, tiled=True)  19.3 us
    psum x1, blocking collectives, shards(): grad_scores = lax.psum(score_part, 'exp')  13.3 us
    reduce_scatter x1, waiting for transfers between devices, shards(): lax.psum_scatter(partial_value, 'exp', scatter_dimension=1, tiled=True)  12.7 us
    gather x1, local copies, waits for them, and re-layouts, shards(): out_grads = jnp.where(mask_send, wide_grads[local], 0)  10.7 us
    gather x1, local copies, waits for them, and re-layouts, shards(): out_rows = jnp.where(mask_send, wide_tokens[local], 0)  10.7 us
  transfers between devices with their start and end apart: 5, of which 5 were waited for; matrix products, arithmetic and copies ran while one was open for 18% of the time, Pallas kernels for 0%

commit v1 on v0

v1 whole, which is shorter than its diff:
```python
import jax
import jax.numpy as jnp
from jax import lax
from jax.sharding import PartitionSpec as P


def send_matrix(chosen, owner_id, tok_dev, most):
    experts, width = chosen.shape
    lower = owner_id * tok_dev
    mine = (chosen >= lower) & (chosen < lower + tok_dev)
    begins = jnp.sum(chosen < lower, axis=1)
    rank = jnp.arange(width, dtype=jnp.int32)[None, :] - begins[:, None]
    slot = jnp.where(mine, rank, -1)
    hit = slot[:, None, :] == jnp.arange(most, dtype=jnp.int32)[None, :, None]
    token = jnp.sum(jnp.where(hit, chosen[:, None, :] - lower + 1, 0), axis=2) - 1
    flat = token.reshape(experts * most, 1)
    return (flat == jnp.arange(tok_dev, dtype=jnp.int32)[None, :]).astype(jnp.bfloat16)


def pick_matrix(picked, owners, tok_dev, most):
    width = picked.shape[0]
    bounds = jnp.arange(owners, dtype=jnp.int32) * tok_dev
    begins = jnp.sum(picked[None, :] < bounds[:, None], axis=1)
    source = picked // tok_dev
    onehot = source[None, :] == jnp.arange(owners, dtype=jnp.int32)[:, None]
    first = jnp.sum(jnp.where(onehot, begins[:, None], 0), axis=0)
    flat = source * most + jnp.arange(width, dtype=jnp.int32) - first
    return (jnp.arange(owners * most, dtype=jnp.int32)[:, None] == flat[None, :]).astype(jnp.bfloat16)


def dot(a, b, ca, cb):
    return lax.dot_general(a, b, (((ca,), (cb,)), ((), ())), preferred_element_type=jnp.float32)


def shards(tokens, grad_out, chosen, scores, gate_weight, up_weight, down_weight):
    owner_id = lax.axis_index("seq")
    owners = lax.axis_size("seq")
    tok_dev, part = tokens.shape
    width = chosen.shape[1]
    most = 2 * width // owners
    bf16 = jnp.bfloat16
    send = send_matrix(chosen, owner_id, tok_dev, most)
    both = jnp.concatenate([tokens, grad_out], axis=1)
    out = dot(send, both, 1, 0).astype(bf16).reshape(owners, most, 2 * part)
    recv = lax.all_to_all(out, "seq", split_axis=0, concat_axis=0, tiled=True)
    picked = lax.dynamic_index_in_dim(chosen, owner_id, 0, keepdims=False)
    pick = pick_matrix(picked, owners, tok_dev, most)
    mine = dot(pick, recv.reshape(owners * most, 2 * part), 0, 0).astype(bf16)
    rows = lax.all_gather(mine[:, :part], "exp", axis=1, tiled=True)
    grads = lax.all_gather(mine[:, part:], "exp", axis=1, tiled=True)
    gains = scores[0]
    gate_mat = gate_weight[0]
    up_mat = up_weight[0]
    down_mat = down_weight[0]
    gate_pre = dot(rows, gate_mat, 1, 0)
    up_pre = dot(rows, up_mat, 1, 0)
    sigma = jax.nn.sigmoid(gate_pre)
    silu_gate = gate_pre * sigma
    hidden = (silu_gate * up_pre).astype(bf16)
    back_hidden = dot(grads, down_mat, 1, 1)
    score_part = jnp.sum(hidden.astype(jnp.float32) * back_hidden, axis=1)
    grad_scores = lax.psum(score_part, "exp")
    scaled = (gains[:, None] * grads.astype(jnp.float32)).astype(bf16)
    hidden_grad = gains[:, None] * back_hidden
    grad_gate_pre = (hidden_grad * up_pre * sigma * (1.0 + gate_pre * (1.0 - sigma))).astype(bf16)
    grad_up_pre = (hidden_grad * silu_gate).astype(bf16)
    partial_value = (dot(grad_gate_pre, gate_mat, 1, 1) + dot(grad_up_pre, up_mat, 1, 1)).astype(bf16)
    summed = lax.psum_scatter(partial_value, "exp", scatter_dimension=1, tiled=True)
    grad_down = dot(hidden, scaled, 0, 0).astype(bf16)
    grad_gate = dot(rows, grad_gate_pre, 0, 0).astype(bf16)
    grad_up = dot(rows, grad_up_pre, 0, 0).astype(bf16)
    outgoing = dot(pick, summed, 1, 0).astype(bf16).reshape(owners, most, part)
    returned = lax.all_to_all(outgoing, "seq", split_axis=0, concat_axis=0, tiled=True)
    total = dot(send, returned.reshape(owners * most, part), 0, 0)
    return (
        total.astype(bf16),
        grad_scores[None, :],
        grad_gate[None],
        grad_up[None],
        grad_down[None],
    )


def solution(mesh):
    in_specs = (
        P("seq", "exp"),
        P("seq", "exp"),
        P(),
        P("seq", None),
        P("seq", None, "exp"),
        P("seq", None, "exp"),
        P("seq", "exp", None),
    )
    out_specs = (
        P("seq", "exp"),
        P("seq", None),
        P("seq", None, "exp"),
        P("seq", None, "exp"),
        P("seq", "exp", None),
    )
    return jax.shard_map(shards, mesh=mesh, in_specs=in_specs, out_specs=out_specs, check_vma=False)
```

time: 308 us -> 172 us (0.56)
  blocking collectives: 71.4 us -> 15.1 us
  local copies, waits for them, and re-layouts: 50.2 us -> 1.09 us
  waiting for transfers between devices: 102 us -> 76.1 us
  other arithmetic: 17 us -> 3.1 us
  matrix products: 40.8 us -> 46.7 us
  starting transfers between devices: 11.7 us -> 15.4 us
    all_to_all x1 -> x0, blocking collectives: 58.1 us -> none  [shards(): lax.all_to_all(out_rows, 'seq', split_axis=0, concat_axis=0, tiled=True)]
    gather x8 -> x0, local copies, waits for them, and re-layouts: 49.1 us -> none  [the longest x1 10.7 us: shards(): out_grads = jnp.where(mask_send, wide_grads[local], 0)]
    all_to_all x1, waiting for transfers between devices: 43.5 us -> 16.6 us  [shards(): recv = lax.all_to_all(out, 'seq', split_axis=0, concat_axis=0, tiled=True)]
    scatter-add x1 -> x0, other arithmetic: 7.2 us -> none  [shards(): total = total.at[local.reshape(-1)].add(contrib.reshape(-1, slice_width))]
    dot_general x8 -> x12, matrix products: 40.8 us -> 46.7 us  [dot(): lax.dot_general(a, b, (((ca,), (cb,)), ((), ())), preferred_element_type=...]
    select_n x8 -> x2, other arithmetic: 6.56 us -> 1.58 us  [the longest x1 0.83 us: send_matrix(): slot = jnp.where(mine, rank, -1)]
    all_gather x2, waiting for transfers between devices: 40 us -> 43.7 us  [the longest x1 23.5 us: shards(): rows = lax.all_gather(mine[:, :part], 'exp', axis=1, tiled=True)]
    all_to_all x1, starting transfers between devices: 4.53 us -> 8.13 us  [shards(): recv = lax.all_to_all(out, 'seq', split_axis=0, concat_axis=0, tiled=True)]
  transfers between devices with their start and end apart: 5 -> 5, of which waited for: 5 -> 5; matrix products, arithmetic and copies ran while one was open for 18% -> 15% of each run, Pallas kernels for 0% -> 0%
where the time goes in v1:
time: 172 us; the launch traced here: 171 us
  waiting for transfers between devices  76.1 us (44%)
  matrix products  46.7 us (27%)
  starting transfers between devices  15.4 us (9%)
  blocking collectives  15.1 us (9%)
  between operations  13.8 us (8%)
  other arithmetic  3.1 us (2%)
    dot_general x12, matrix products, dot(): lax.dot_general(a, b, (((ca,), (cb,)), ((), ())), preferred_element_type=...  46.7 us
    all_gather x1, waiting for transfers between devices, shards(): rows = lax.all_gather(mine[:, :part], 'exp', axis=1, tiled=True)  23.5 us
    all_gather x1, waiting for transfers between devices, shards(): grads = lax.all_gather(mine[:, part:], 'exp', axis=1, tiled=True)  20.2 us
    all_to_all x1, waiting for transfers between devices, shards(): recv = lax.all_to_all(out, 'seq', split_axis=0, concat_axis=0, tiled=True)  16.6 us
    psum x1, blocking collectives, shards(): grad_scores = lax.psum(score_part, 'exp')  15.1 us
    reduce_scatter x1, waiting for transfers between devices, shards(): lax.psum_scatter(partial_value, 'exp', scatter_dimension=1, tiled=True)  10.6 us
    all_to_all x1, starting transfers between devices, shards(): recv = lax.all_to_all(out, 'seq', split_axis=0, concat_axis=0, tiled=True)  8.13 us
    all_to_all x1, starting transfers between devices, shards(): lax.all_to_all(outgoing, 'seq', split_axis=0, concat_axis=0, tiled=True)  6.96 us
  transfers between devices with their start and end apart: 5, of which 5 were waited for; matrix products, arithmetic and copies ran while one was open for 15% of the time, Pallas kernels for 0%

profile of v1, /device:TPU:0, one launch (start us, length us, event | category | flops | bytes accessed | tf_op | source)
XLA Modules:
  0.0 171.3 jit_solution(8608244515244887630)
XLA Ops:
  7.2 0.9 convert_reduce_fusion.1
  8.0 0.8 subtract_select_fusion
  8.9 0.4 select_reduce_fusion
  9.3 0.1 sub.42
  9.3 2.8 %fusion.18 = bf16[1024,512]{1,0:T(8,128)(2,1)} fusion(s32[1024]{0:T(1024)S(1)} %sub.42, bf16[512,256]{1,0:T(8,128)(2,1)} %param.8, bf16[512,256]{1,0:T(8,128)(2,1)} %param.7), kind=kOutput, calls=%fused_computation.30 | convolution fusion | flops 538968064 | bytes 1576960 | tf_op jit(solution)/shard_map/dot_general | solution.py:32
  12.1 8.1 %all-to-all-start = ((bf16[16,64,512]{2,1,0:T(8,128)(2,1)}), bf16[16,64,512]{2,1,0:T(8,128)(2,1)S(1)}, u32[]{:S(2)}, u32[]{:S(2)}) async-start(bf16[16,64,512]{2,1,0:T(8,128)(2,1)} %bitcast.5), calls=%async_computation | async-start | bytes 2097152 | tf_op jit(solution)/shard_map/all_to_all | solution.py:45
  20.2 0.0 all-gather.5.cloned.1.call-start
  20.3 0.7 and_select_fusion
  21.0 0.2 convert_reduce_fusion
  21.2 0.1 select_reduce_fusion.1
  21.3 16.6 %all-to-all-done = bf16[16,64,512]{2,1,0:T(8,128)(2,1)S(1)} async-done(((bf16[16,64,512]{2,1,0:T(8,128)(2,1)}), bf16[16,64,512]{2,1,0:T(8,128)(2,1)S(1)}, u32[]{:S(2)}, u32[]{:S(2)}) %all-to-all-start) | async-done | bytes 1048608 | tf_op jit(solution)/shard_map/all_to_all | solution.py:45
  37.9 0.8 fusion.19
  38.6 0.8 fusion.30
  39.5 0.7 all-gather.3.cloned.1.call-update
  40.2 0.2 reduce-scatter.2.cloned.1.call-start
  40.5 23.5 %all-gather.5.cloned.1.call-done = bf16[512,2048]{1,0:T(8,128)(2,1)} async-done(((bf16[512,256]{1,0:T(8,128)(2,1)}), bf16[512,2048]{1,0:T(8,128)(2,1)}) %all-gather.5.cloned.1.call-update) | async-done | bytes 2097168 | tf_op jit(solution)/shard_map/all_gather | solution.py:49
  64.0 6.6 %fusion.6 = f32[512,1024]{1,0:T(8,128)} fusion(bf16[512,2048]{1,0:T(8,128)(2,1)} %all-gather.5.cloned.1.call-done, bf16[1,2048,1024]{2,1,0:T(8,128)(2,1)} %param.12), kind=kOutput, calls=%fused_computation.6 | convolution fusion | flops 2147483648 | bytes 8388608 | tf_op jit(solution)/shard_map/dot_general | solution.py:32
  70.6 3.7 %fusion.2 = f32[512,1024]{1,0:T(8,128)} fusion(bf16[512,2048]{1,0:T(8,128)(2,1)S(1)} %copy-done.3, bf16[1,2048,1024]{2,1,0:T(8,128)(2,1)S(1)} %copy-done), kind=kOutput, calls=%fused_computation.2 | convolution fusion | flops 2147483648 | bytes 8388608 | tf_op jit(solution)/shard_map/dot_general | solution.py:32
  74.2 20.2 %all-gather.3.cloned.1.call-done = bf16[512,2048]{1,0:T(8,128)(2,1)} async-done(((bf16[512,256]{1,0:T(8,128)(2,1)}), bf16[512,2048]{1,0:T(8,128)(2,1)}) %all-gather.3.cloned.1.call-update) | async-done | bytes 2097168 | tf_op jit(solution)/shard_map/all_gather | solution.py:50
  94.5 8.4 %multiply_reduce_fusion = (f32[512]{0:T(512)S(1)}, bf16[512,1024]{1,0:T(8,128)(2,1)}, bf16[512,1024]{1,0:T(8,128)(2,1)S(1)}, bf16[512,1024]{1,0:T(8,128)(2,1)S(1)}) fusion(f32[512,1024]{1,0:T(8,128)} %fusion.6, f32[512,1024]{1,0:T(8,128)} %fusion.2, f32[512]{0:T(512)S(1)} %bitcast.54, bf16[512,2048]{1,0:T(8,128)(2,1)} %all-gather.3.cloned.1.call-done, ...), kind=kOutput, calls=%fused_computation.16 | convolution fusion | flops 2157444608 | bytes 13635584 | tf_op jit(solution)/shard_map/dot_general | solution.py:32
  102.9 2.4 %fusion = f32[512,2048]{1,0:T(8,128)S(1)} fusion(bf16[512,1024]{1,0:T(8,128)(2,1)S(1)} %get-tuple-element.9, bf16[1,2048,1024]{2,1,0:T(8,128)(2,1)S(1)} %copy-done.1), kind=kOutput, calls=%fused_computation | convolution fusion | flops 2147483648 | bytes 9437184 | tf_op jit(solution)/shard_map/dot_general | solution.py:32
  105.2 0.2 copy-done.2
  105.4 3.7 %add_convert_fusion = bf16[512,2048]{1,0:T(8,128)(2,1)} fusion(f32[512,2048]{1,0:T(8,128)S(1)} %fusion, bf16[512,1024]{1,0:T(8,128)(2,1)S(1)} %get-tuple-element.10, bf16[1,2048,1024]{2,1,0:T(8,128)(2,1)S(1)} %copy-done.2), kind=kOutput, calls=%fused_computation.14 | convolution fusion | flops 2149580800 | bytes 11534336 | tf_op jit(solution)/shard_map/dot_general | solution.py:32
  109.1 15.1 %psum.7 = f32[1,512]{1,0:T(1,128)} all-reduce(f32[1,512]{1,0:T(1,128)S(1)} %bitcast.53), channel_id=1, replica_groups=mesh['seq'=16,'exp'=8] {'exp'}, use_global_device_ids=true, to_apply=%region_6.7 | all-reduce | flops 512 | bytes 4096 | tf_op jit(solution)/shard_map/psum | solution.py:62
  124.3 4.4 %convert_bitcast_fusion.2 = bf16[1,2048,1024]{2,1,0:T(8,128)(2,1)} fusion(bf16[512,2048]{1,0:T(8,128)(2,1)S(1)} %copy-done.3, bf16[512,1024]{1,0:T(8,128)(2,1)S(1)} %get-tuple-element.9), kind=kOutput, calls=%fused_computation.13 | convolution fusion | flops 2149580800 | bytes 7340032 | tf_op jit(solution)/shard_map/dot_general | solution.py:32
  128.7 4.6 %convert_bitcast_fusion = bf16[1,1024,2048]{2,1,0:T(8,128)(2,1)} fusion(bf16[512,1024]{1,0:T(8,128)(2,1)S(1)} %copy-done.7, bf16[512,2048]{1,0:T(8,128)(2,1)S(1)} %copy-done.4, f32[512]{0:T(512)S(1)} %bitcast.55), kind=kOutput, calls=%fused_computation.10 | convolution fusion | flops 2152726528 | bytes 7342080 | tf_op jit(solution)/shard_map/dot_general | solution.py:32
  133.2 10.6 %reduce-scatter.2.cloned.1.call-done = bf16[512,256]{1,0:T(8,128)(2,1)} async-done(((bf16[512,2048]{1,0:T(8,128)(2,1)}), bf16[512,256]{1,0:T(8,128)(2,1)}) %reduce-scatter.2.cloned.1.call-update) | async-done | bytes 262160 | tf_op jit(solution)/shard_map/reduce_scatter | solution.py:68
  143.9 2.2 %fusion.20 = bf16[1024,256]{1,0:T(8,128)(2,1)} fusion(bf16[512,256]{1,0:T(8,128)(2,1)} %reduce-scatter.2.cloned.1.call-done, s32[512]{0:T(512)S(1)} %bitcast.52), kind=kOutput, calls=%fused_computation.32 | convolution fusion | flops 269221888 | bytes 788480 | tf_op jit(solution)/shard_map/dot_general | solution.py:32
  146.1 7.0 %all-to-all-start.1 = ((bf16[16,64,256]{2,1,0:T(8,128)(2,1)}), bf16[16,64,256]{2,1,0:T(8,128)(2,1)S(1)}, u32[]{:S(2)}, u32[]{:S(2)}) async-start(bf16[16,64,256]{2,1,0:T(8,128)(2,1)} %bitcast.10), calls=%async_computation.2 | async-start | bytes 1048576 | tf_op jit(solution)/shard_map/all_to_all | solution.py:73
  153.1 5.6 %convert_bitcast_fusion.1 = bf16[1,2048,1024]{2,1,0:T(8,128)(2,1)} fusion(bf16[512,2048]{1,0:T(8,128)(2,1)S(1)} %copy-done.3, bf16[512,1024]{1,0:T(8,128)(2,1)} %copy-done.6), kind=kOutput, calls=%fused_computation.12 | convolution fusion | flops 2149580800 | bytes 7340032 | tf_op jit(solution)/shard_map/dot_general | solution.py:32
  158.7 4.5 %all-to-all-done.1 = bf16[16,64,256]{2,1,0:T(8,128)(2,1)S(1)} async-done(((bf16[16,64,256]{2,1,0:T(8,128)(2,1)}), bf16[16,64,256]{2,1,0:T(8,128)(2,1)S(1)}, u32[]{:S(2)}, u32[]{:S(2)}) %all-to-all-start.1) | async-done | bytes 524320 | tf_op jit(solution)/shard_map/all_to_all | solution.py:73
  163.2 1.6 fusion.21
  (21 shorter events, 0.1 us)
Async XLA Ops:
  12.1 25.8 %all-to-all-start = ((bf16[16,64,512]{2,1,0:T(8,128)(2,1)}), bf16[16,64,512]{2,1,0:T(8,128)(2,1)S(1)}, u32[]{:S(2)}, u32[]{:S(2)}) async-start(bf16[16,64,512]{2,1,0:T(8,128)(2,1)} %bitcast.5), calls=%async_computation | async-start | bytes 2097152 | tf_op jit(solution)/shard_map/all_to_all | solution.py:45
  20.2 43.7 %all-gather.5.cloned.1.call-start = ((), (), s32[]{:S(2)}) async-start(), calls=%async_computation.4 | async-start | bytes 2359296 | tf_op jit(solution)/shard_map/all_gather | solution.py:49
  39.5 55.0 %all-gather.3.cloned.1.call-start = ((), (), s32[]{:S(2)}) async-start(), calls=%async_computation.3 | async-start | bytes 2359296 | tf_op jit(solution)/shard_map/all_gather | solution.py:50
  40.2 103.7 %reduce-scatter.2.cloned.1.call-start = ((), (), s32[]{:S(2)}) async-start(), calls=%async_computation.5 | async-start | bytes 2359296 | tf_op jit(solution)/shard_map/reduce_scatter | solution.py:68
  63.9 6.6 %copy-start = (bf16[1,2048,1024]{2,1,0:T(8,128)(2,1)S(1)}, bf16[1,2048,1024]{2,1,0:T(8,128)(2,1)}, u32[]{:S(2)}) copy-start(bf16[1,2048,1024]{2,1,0:T(8,128)(2,1)} %param.11) | copy-start | bytes 12582916
  64.0 6.6 %copy-start.3 = (bf16[512,2048]{1,0:T(8,128)(2,1)S(1)}, bf16[512,2048]{1,0:T(8,128)(2,1)}, u32[]{:S(2)}) copy-start(bf16[512,2048]{1,0:T(8,128)(2,1)} %all-gather.5.cloned.1.call-done) | copy-start | bytes 6291460
  70.6 23.9 %copy-start.5 = (f32[1,512]{1,0:T(1,128)S(1)}, f32[1,512]{1,0:T(1,128)}, u32[]{:S(2)}) copy-start(f32[1,512]{1,0:T(1,128)} %param.10) | copy-start | bytes 6148
  94.4 8.4 %copy-start.1 = (bf16[1,2048,1024]{2,1,0:T(8,128)(2,1)S(1)}, bf16[1,2048,1024]{2,1,0:T(8,128)(2,1)}, u32[]{:S(2)}) copy-start(bf16[1,2048,1024]{2,1,0:T(8,128)(2,1)} %param.11) | copy-start | bytes 12582916
  102.8 2.4 %copy-start.6 = (bf16[512,1024]{1,0:T(8,128)(2,1)}, bf16[512,1024]{1,0:T(8,128)(2,1)S(1)}, u32[]{:S(2)}) copy-start(bf16[512,1024]{1,0:T(8,128)(2,1)S(1)} %get-tuple-element.10) | copy-start | bytes 3145732
  102.8 2.6 %copy-start.2 = (bf16[1,2048,1024]{2,1,0:T(8,128)(2,1)S(1)}, bf16[1,2048,1024]{2,1,0:T(8,128)(2,1)}, u32[]{:S(2)}) copy-start(bf16[1,2048,1024]{2,1,0:T(8,128)(2,1)} %param.12) | copy-start | bytes 12582916
  124.3 4.4 %copy-start.4 = (bf16[512,2048]{1,0:T(8,128)(2,1)S(1)}, bf16[512,2048]{1,0:T(8,128)(2,1)}, u32[]{:S(2)}) copy-start(bf16[512,2048]{1,0:T(8,128)(2,1)} %all-gather.3.cloned.1.call-done) | copy-start | bytes 6291460
  124.3 4.4 %copy-start.7 = (bf16[512,1024]{1,0:T(8,128)(2,1)S(1)}, bf16[512,1024]{1,0:T(8,128)(2,1)}, u32[]{:S(2)}) copy-start(bf16[512,1024]{1,0:T(8,128)(2,1)} %get-tuple-element.6) | copy-start | bytes 3145732
  146.1 17.1 %all-to-all-start.1 = ((bf16[16,64,256]{2,1,0:T(8,128)(2,1)}), bf16[16,64,256]{2,1,0:T(8,128)(2,1)S(1)}, u32[]{:S(2)}, u32[]{:S(2)}) async-start(bf16[16,64,256]{2,1,0:T(8,128)(2,1)} %bitcast.10), calls=%async_computation.2 | async-start | bytes 1048576 | tf_op jit(solution)/shard_map/all_to_all | solution.py:73
Sparse Core Ops, SparseCore 0:
  39.6 24.3 all-gather.4
  66.2 28.2 all-gather.2
  109.2 34.5 reduce-scatter.1

commit v2 on v1

v2 whole, which is shorter than its diff:
```python
import functools

import jax
import jax.numpy as jnp
from jax import lax
from jax.experimental import pallas as pl
from jax.experimental.pallas import tpu as pltpu
from jax.sharding import PartitionSpec as P

MESH = pl.DeviceIdType.MESH
BF16 = jnp.bfloat16
F32 = jnp.float32

OWNERS = 16
MOST = 64
CAP = 512
PART = 256
CHIPS = 4
WIDE = 512
HID = 1024
HALF = CAP // 2
VMEM_BYTES = 60 * 1024 * 1024


def dot(a, b):
    return jnp.dot(a, b, preferred_element_type=F32)


def dot_t(a, b):
    return lax.dot_general(a, b, (((1,), (1,)), ((), ())), preferred_element_type=F32)


def iota(shape, axis):
    return lax.broadcasted_iota(jnp.int32, shape, axis)


def part_of(c):
    return pl.ds(pl.multiple_of(c * PART, PART), PART)


def layer_kernel(
    tokens, grads_in, chosen, scores, gate_hbm, up_hbm, down_hbm,
    tok_out, score_out, rows_t_hbm, scaled_hbm, hidden_t_hbm, ggp_hbm, gup_hbm,
    gate_v, up_v, down_v, full, gate_acc, up_acc, back_acc, hidden, hidden_t, ggp, gup,
    rows_t, send_m, send_t, pick_m, pick_t, out_x, in_x, out_r, in_r, sums, sib_out, sib_in,
    rel_out, rel_in, dir_out, dir_in, fin_out, fin_in, score_buf, gain_col,
    w_sem, o_sem, x_send, x_recv, g_send, g_recv, s_send, s_recv, c_send, c_recv, r_send, r_recv,
    q_send, q_recv,
):
    seq = lax.axis_index("seq")
    ex = lax.axis_index("exp")
    zz, yy = seq // 4, lax.rem(seq, 4)
    x, c = ex // 2, lax.rem(ex, 2)
    right, left, opp = lax.rem(x + 1, 4), lax.rem(x + 3, 4), lax.rem(x + 2, 4)
    oc = 1 - c

    def seq_peer(k):
        dz, dy = k // 4, lax.rem(k, 4)
        return lax.rem(zz + dz, 4) * 4 + lax.rem(yy + dy, 4)

    weight_copies = [
        pltpu.make_async_copy(gate_hbm, gate_v, w_sem.at[0]),
        pltpu.make_async_copy(up_hbm, up_v, w_sem.at[1]),
    ] + [
        pltpu.make_async_copy(down_hbm.at[0, :, pl.ds(i * WIDE, WIDE)], down_v.at[i], w_sem.at[2 + i])
        for i in range(CHIPS)
    ]
    for copy in weight_copies:
        copy.start()

    barrier = pltpu.get_barrier_semaphore()

    def greet_seq(k, carry):
        pl.semaphore_signal(barrier, inc=1, device_id=(seq_peer(k), ex), device_id_type=MESH)
        return carry

    def greet_exp(k, carry):
        pl.semaphore_signal(barrier, inc=1, device_id=(seq, lax.rem(ex + k, 8)), device_id_type=MESH)
        return carry

    lax.fori_loop(1, OWNERS, greet_seq, 0)
    lax.fori_loop(1, 8, greet_exp, 0)

    lane = iota((1, CAP), 1)
    lower = seq * CAP
    table = chosen[...]
    begins = jnp.sum((table < lower).astype(jnp.int32), axis=1, keepdims=True)
    mine = jnp.logical_and(table >= lower, table < lower + CAP)
    slots = jnp.where(mine, iota((OWNERS, CAP), 1) - begins, -1)
    local = table - lower
    sub = iota((MOST, CAP), 0)
    lanes = iota((MOST, CAP), 1)
    for e in range(OWNERS):
        hit = slots[e : e + 1, :] == sub
        token = jnp.sum(jnp.where(hit, local[e : e + 1, :] + 1, 0), axis=1, keepdims=True) - 1
        send_m[e * MOST : (e + 1) * MOST, :] = jnp.where(token == lanes, 1.0, 0.0).astype(BF16)
    out_x[0] = dot(send_m[...], tokens[...]).astype(BF16)

    def x_copy(a, peer, slot):
        return pltpu.make_async_remote_copy(
            src_ref=out_x.at[a, pl.ds(pl.multiple_of(peer * MOST, MOST), MOST), :],
            dst_ref=in_x.at[a, pl.ds(pl.multiple_of(slot * MOST, MOST), MOST), :],
            send_sem=x_send.at[a, peer],
            recv_sem=x_recv.at[a, slot],
            device_id=(peer, ex),
            device_id_type=MESH,
        )

    def x_start(a):
        def body(k, carry):
            x_copy(a, seq_peer(k), seq).start()
            return carry

        lax.fori_loop(1, OWNERS, body, 0)
        here = pl.ds(pl.multiple_of(seq * MOST, MOST), MOST)
        in_x[a, here, :] = out_x[a, here, :]

    def x_wait(a):
        def body(k, carry):
            peer = seq_peer(k)
            x_copy(a, peer, peer).wait_recv()
            return carry

        lax.fori_loop(1, OWNERS, body, 0)

    pl.semaphore_wait(barrier, OWNERS - 1 + 7)
    x_start(0)
    out_x[1] = dot(send_m[...], grads_in[...]).astype(BF16)
    x_start(1)

    picked = chosen[pl.ds(seq, 1), :]
    owner_low = iota((OWNERS, CAP), 0) * CAP
    wide = jnp.broadcast_to(picked, (OWNERS, CAP))
    firsts = jnp.sum((wide < owner_low).astype(jnp.int32), axis=1, keepdims=True)
    inside = jnp.logical_and(wide >= owner_low, wide < owner_low + CAP)
    places = jnp.where(inside, iota((OWNERS, CAP), 1) - firsts, -1)
    for g in range(OWNERS // 2):
        block = jnp.concatenate(
            [jnp.where(places[o : o + 1, :] == sub, 1.0, 0.0) for o in (2 * g, 2 * g + 1)], axis=0
        )
        here = slice(g * 2 * MOST, (g + 1) * 2 * MOST)
        pick_t[here, :] = block.astype(BF16)
        pick_m[:, here] = block.T.astype(BF16)
    gain_col[...] = jnp.broadcast_to(scores[...], (128, CAP)).T

    def piece(a, xx, cc, half=None):
        rows = slice(None) if half is None else pl.ds(half * HALF, HALF)
        return full.at[a, xx, rows, part_of(cc)]

    def g_copy(a, k):
        view, target = {
            0: (piece(a, x, c), (x, oc)),
            1: (piece(a, x, c), (right, c)),
            2: (piece(a, x, c), (left, c)),
            3: (piece(a, left, c), (x, oc)),
            4: (piece(a, right, c), (x, oc)),
            5: (piece(a, left, c, 0), (right, c)),
            6: (piece(a, right, c, 1), (left, c)),
            7: (piece(a, opp, c, 0), (x, oc)),
            8: (piece(a, opp, c, 1), (x, oc)),
        }[k]
        return pltpu.make_async_remote_copy(
            src_ref=view, dst_ref=view, send_sem=g_send.at[a, k], recv_sem=g_recv.at[a, k],
            device_id=(seq, target[0] * 2 + target[1]), device_id_type=MESH,
        )

    def g_wait(a, *ks):
        for k in ks:
            g_copy(a, k).wait_recv()

    def g_start(a, *ks):
        for k in ks:
            g_copy(a, k).start()

    def compact(a):
        x_wait(a)
        full[a, x, :, part_of(c)] = dot(pick_m[...], in_x[a]).astype(BF16)
        g_start(a, 1, 2, 0)

    def gate_up(xx, first):
        def body(n, carry):
            cols = pl.ds(pl.multiple_of(n * WIDE, WIDE), WIDE)
            for acc, w in ((gate_acc, gate_v), (up_acc, up_v)):
                term = dot(full[0, xx], w[xx, :, cols])
                acc[:, cols] = term if first else acc[:, cols] + term
            return carry

        lax.fori_loop(0, HID // WIDE, body, 0)

    def flip_rows(xx):
        rows_t[xx] = full[0, xx].T
        pltpu.make_async_copy(rows_t.at[xx], rows_t_hbm.at[xx], o_sem.at[0, xx]).start()

    def back(xx, first):
        def body(n, carry):
            cols = pl.ds(pl.multiple_of(n * WIDE, WIDE), WIDE)
            term = dot_t(full[1, xx], down_v[xx, cols, :])
            back_acc[:, cols] = term if first else back_acc[:, cols] + term
            return carry

        lax.fori_loop(0, HID // WIDE, body, 0)

    compact(0)
    for copy in weight_copies[:2]:
        copy.wait()
    compact(1)
    g_wait(0, 0)
    gate_up(x, True)
    g_wait(0, 1)
    g_start(0, 5, 3)
    g_wait(0, 2)
    g_start(0, 6, 4)
    flip_rows(x)
    g_wait(0, 3)
    gate_up(left, False)
    g_wait(0, 4)
    gate_up(right, False)
    g_wait(0, 5, 6)
    g_start(0, 7, 8)
    for copy in weight_copies[2:]:
        copy.wait()
    g_wait(1, 0)
    back(x, True)
    g_wait(1, 1)
    g_start(1, 5, 3)
    g_wait(1, 2)
    g_start(1, 6, 4)
    g_wait(0, 7, 8)
    gate_up(opp, False)

    def activate(i, carry):
        rows = pl.ds(pl.multiple_of(i * 16, 16), 16)
        pre, up = gate_acc[rows, :], up_acc[rows, :]
        sigma = jax.nn.sigmoid(pre)
        silu = pre * sigma
        hidden[rows, :] = (silu * up).astype(BF16)
        gate_acc[rows, :] = up * sigma * (1.0 + pre * (1.0 - sigma))
        up_acc[rows, :] = silu
        return carry

    lax.fori_loop(0, CAP // 16, activate, 0)
    flip_rows(left)
    g_wait(1, 3)
    back(left, False)
    g_wait(1, 4)
    back(right, False)
    flip_rows(right)
    g_wait(1, 5, 6)
    g_start(1, 7, 8)
    flip_rows(opp)
    hidden_t[...] = hidden[...].T
    hidden_copy = pltpu.make_async_copy(hidden_t, hidden_t_hbm, o_sem.at[2, 0])
    hidden_copy.start()

    g_wait(1, 7, 8)
    back(opp, False)

    def finish(i, carry):
        rows = pl.ds(pl.multiple_of(i * 16, 16), 16)
        bh = back_acc[rows, :]
        gain = gain_col[rows, 0:1]
        dh = gain * bh
        ggp[rows, :] = (dh * gate_acc[rows, :]).astype(BF16)
        gup[rows, :] = (dh * up_acc[rows, :]).astype(BF16)
        prod = hidden[rows, :].astype(F32) * bh
        part = prod[:, 0:128]
        for j in range(1, HID // 128):
            part = part + prod[:, j * 128 : (j + 1) * 128]
        back_acc[rows, 0:128] = part
        return carry

    lax.fori_loop(0, CAP // 16, finish, 0)
    grad_copies = [
        pltpu.make_async_copy(ggp, ggp_hbm, o_sem.at[2, 1]),
        pltpu.make_async_copy(gup, gup_hbm, o_sem.at[2, 2]),
    ]
    for copy in grad_copies:
        copy.start()

    def contrib(xx, cc):
        feats = part_of(cc)
        return dot_t(ggp[...], gate_v[xx, feats, :]) + dot_t(gup[...], up_v[xx, feats, :])

    def s_copy(k, xx):
        return pltpu.make_async_remote_copy(
            src_ref=sib_out.at[xx], dst_ref=sib_in.at[xx], send_sem=s_send.at[k], recv_sem=s_recv.at[k],
            device_id=(seq, x * 2 + oc), device_id_type=MESH,
        )

    def r_copy(k):
        src, dst, target = (
            (rel_out.at[0], rel_in.at[0], right),
            (rel_out.at[1], rel_in.at[1], left),
            (dir_out.at[0], dir_in.at[0], right),
            (dir_out.at[1], dir_in.at[1], left),
            (fin_out.at[0], fin_in.at[0], right),
            (fin_out.at[1], fin_in.at[1], left),
        )[k]
        return pltpu.make_async_remote_copy(
            src_ref=src, dst_ref=dst, send_sem=r_send.at[k], recv_sem=r_recv.at[k],
            device_id=(seq, target * 2 + c), device_id_type=MESH,
        )

    order = (opp, right, left, x)

    def for_sibling(k):
        sib_out[order[k]] = contrib(order[k], oc).astype(BF16)
        s_copy(k, order[k]).start()

    def for_chip(k):
        sums[k] = contrib(order[k], c)

    def add_sibling(k):
        s_copy(k, order[k]).wait_recv()
        sums[k] = sums[k] + sib_in[order[k]].astype(F32)

    for_sibling(0)
    for_sibling(1)
    for_chip(0)
    add_sibling(0)
    rel_out[0] = sums[0, 0:HALF, :].astype(BF16)
    rel_out[1] = sums[0, HALF:CAP, :].astype(BF16)
    r_copy(0).start()
    r_copy(1).start()
    for_sibling(2)
    for_chip(1)
    add_sibling(1)
    dir_out[0] = sums[1, HALF:CAP, :].astype(BF16)
    r_copy(2).start()
    for_chip(2)
    add_sibling(2)
    dir_out[1] = sums[2, 0:HALF, :].astype(BF16)
    r_copy(3).start()
    for_sibling(3)

    score_part = jnp.sum(back_acc[:, 0:128].T, axis=0, keepdims=True)
    score_buf[ex] = jnp.broadcast_to(score_part, (8, CAP))

    def q_copy(peer, slot):
        return pltpu.make_async_remote_copy(
            src_ref=score_buf.at[ex], dst_ref=score_buf.at[slot], send_sem=q_send.at[peer], recv_sem=q_recv.at[slot],
            device_id=(seq, peer), device_id_type=MESH,
        )

    def q_start(k, carry):
        q_copy(lax.rem(ex + k, 8), ex).start()
        return carry

    r_copy(0).wait_recv()
    fin_out[0] = (sums[1, 0:HALF, :] + rel_in[0].astype(F32)).astype(BF16)
    r_copy(4).start()
    r_copy(1).wait_recv()
    fin_out[1] = (sums[2, HALF:CAP, :] + rel_in[1].astype(F32)).astype(BF16)
    r_copy(5).start()
    lax.fori_loop(1, 8, q_start, 0)
    for_chip(3)
    add_sibling(3)

    for k in range(9):
        g_copy(1, k).wait_send()
    for i in range(CHIPS):
        gain = gain_col[:, 0:1]
        full[1, i] = (gain * full[1, i].astype(F32)).astype(BF16)
        pltpu.make_async_copy(full.at[1, i], scaled_hbm.at[i], o_sem.at[1, i]).start()

    for k in (2, 3, 4, 5):
        r_copy(k).wait_recv()
    low = sums[3, 0:HALF, :] + fin_in[0].astype(F32) + dir_in[1].astype(F32)
    high = sums[3, HALF:CAP, :] + dir_in[0].astype(F32) + fin_in[1].astype(F32)
    summed = jnp.concatenate([low.astype(BF16), high.astype(BF16)], axis=0)
    out_r[...] = dot(pick_t[...], summed).astype(BF16)

    def c_copy(peer, slot):
        return pltpu.make_async_remote_copy(
            src_ref=out_r.at[pl.ds(pl.multiple_of(peer * MOST, MOST), MOST), :],
            dst_ref=in_r.at[pl.ds(pl.multiple_of(slot * MOST, MOST), MOST), :],
            send_sem=c_send.at[peer],
            recv_sem=c_recv.at[slot],
            device_id=(peer, ex),
            device_id_type=MESH,
        )

    def c_start(k, carry):
        c_copy(seq_peer(k), seq).start()
        return carry

    def c_wait(k, carry):
        peer = seq_peer(k)
        c_copy(peer, peer).wait_recv()
        return carry

    lax.fori_loop(1, OWNERS, c_start, 0)
    here = pl.ds(pl.multiple_of(seq * MOST, MOST), MOST)
    in_r[here, :] = out_r[here, :]

    for g in range(OWNERS // 2):
        here = slice(g * 2 * MOST, (g + 1) * 2 * MOST)
        send_t[:, here] = send_m[here, :].astype(F32).T.astype(BF16)

    def q_wait(k, carry):
        peer = lax.rem(ex + k, 8)
        q_copy(peer, peer).wait_recv()
        return carry

    lax.fori_loop(1, 8, q_wait, 0)
    total = score_buf[0, 0:1, :]
    for i in range(1, 8):
        total = total + score_buf[i, 0:1, :]
    score_out[...] = total

    lax.fori_loop(1, OWNERS, c_wait, 0)
    tok_out[...] = dot(send_t[...], in_r[...]).astype(BF16)

    def sent(k, carry):
        peer = seq_peer(k)
        x_copy(0, peer, seq).wait_send()
        x_copy(1, peer, seq).wait_send()
        c_copy(peer, seq).wait_send()
        return carry

    def q_sent(k, carry):
        q_copy(lax.rem(ex + k, 8), ex).wait_send()
        return carry

    lax.fori_loop(1, OWNERS, sent, 0)
    lax.fori_loop(1, 8, q_sent, 0)
    for k in range(9):
        g_copy(0, k).wait_send()
    for k in range(4):
        s_copy(k, order[k]).wait_send()
    for k in range(6):
        r_copy(k).wait_send()
    for i in range(CHIPS):
        pltpu.make_async_copy(rows_t.at[i], rows_t_hbm.at[i], o_sem.at[0, i]).wait()
        pltpu.make_async_copy(full.at[1, i], scaled_hbm.at[i], o_sem.at[1, i]).wait()
    hidden_copy.wait()
    for copy in grad_copies:
        copy.wait()


def weight_kernel(rows_t, scaled, hidden_t, ggp, gup, grad_gate, grad_up, grad_down):
    grad_gate[...] = dot(rows_t[...], ggp[...]).astype(BF16)
    grad_up[...] = dot(rows_t[...], gup[...]).astype(BF16)
    grad_down[...] = dot(hidden_t[...], scaled[...]).astype(BF16)


def shards(tokens, grad_out, chosen, scores, gate_weight, up_weight, down_weight):
    vmem = pl.BlockSpec(memory_space=pltpu.VMEM)
    anyw = pl.BlockSpec(memory_space=pl.ANY)
    shape = jax.ShapeDtypeStruct
    dma = pltpu.SemaphoreType.DMA
    tok, score, rows_t, scaled, hidden_t, ggp, gup = pl.pallas_call(
        layer_kernel,
        out_shape=(
            shape((CAP, PART), BF16),
            shape((1, CAP), F32),
            shape((CHIPS, WIDE, CAP), BF16),
            shape((CHIPS, CAP, WIDE), BF16),
            shape((HID, CAP), BF16),
            shape((CAP, HID), BF16),
            shape((CAP, HID), BF16),
        ),
        in_specs=[vmem] * 4 + [anyw] * 3,
        out_specs=(vmem, vmem) + (anyw,) * 5,
        scratch_shapes=[
            pltpu.VMEM((CHIPS, WIDE, HID), BF16),
            pltpu.VMEM((CHIPS, WIDE, HID), BF16),
            pltpu.VMEM((CHIPS, HID, WIDE), BF16),
            pltpu.VMEM((2, CHIPS, CAP, WIDE), BF16),
            pltpu.VMEM((CAP, HID), F32),
            pltpu.VMEM((CAP, HID), F32),
            pltpu.VMEM((CAP, HID), F32),
            pltpu.VMEM((CAP, HID), BF16),
            pltpu.VMEM((HID, CAP), BF16),
            pltpu.VMEM((CAP, HID), BF16),
            pltpu.VMEM((CAP, HID), BF16),
            pltpu.VMEM((CHIPS, WIDE, CAP), BF16),
            pltpu.VMEM((OWNERS * MOST, CAP), BF16),
            pltpu.VMEM((CAP, OWNERS * MOST), BF16),
            pltpu.VMEM((CAP, OWNERS * MOST), BF16),
            pltpu.VMEM((OWNERS * MOST, CAP), BF16),
            pltpu.VMEM((2, OWNERS * MOST, PART), BF16),
            pltpu.VMEM((2, OWNERS * MOST, PART), BF16),
            pltpu.VMEM((OWNERS * MOST, PART), BF16),
            pltpu.VMEM((OWNERS * MOST, PART), BF16),
            pltpu.VMEM((CHIPS, CAP, PART), F32),
            pltpu.VMEM((CHIPS, CAP, PART), BF16),
            pltpu.VMEM((CHIPS, CAP, PART), BF16),
        ]
        + [pltpu.VMEM((2, HALF, PART), BF16)] * 6
        + [
            pltpu.VMEM((8, 8, CAP), F32),
            pltpu.VMEM((CAP, 128), F32),
            dma((2 + CHIPS,)),
            dma((3, CHIPS)),
            dma((2, OWNERS)),
            dma((2, OWNERS)),
            dma((2, 9)),
            dma((2, 9)),
            dma((4,)),
            dma((4,)),
            dma((OWNERS,)),
            dma((OWNERS,)),
            dma((6,)),
            dma((6,)),
            dma((8,)),
            dma((8,)),
        ],
        compiler_params=pltpu.CompilerParams(
            collective_id=0, has_side_effects=True, vmem_limit_bytes=VMEM_BYTES
        ),
        name="layer",
    )(
        tokens,
        grad_out,
        chosen,
        scores,
        gate_weight.reshape(CHIPS, WIDE, HID),
        up_weight.reshape(CHIPS, WIDE, HID),
        down_weight,
    )
    whole = lambda i: (0, 0)
    none = pl.squeezed
    grad_gate, grad_up, grad_down = pl.pallas_call(
        weight_kernel,
        grid=(CHIPS,),
        out_shape=(
            shape((1, CHIPS * WIDE, HID), BF16),
            shape((1, CHIPS * WIDE, HID), BF16),
            shape((1, HID, CHIPS * WIDE), BF16),
        ),
        in_specs=[
            pl.BlockSpec((none, WIDE, CAP), lambda i: (i, 0, 0)),
            pl.BlockSpec((none, CAP, WIDE), lambda i: (i, 0, 0)),
            pl.BlockSpec((HID, CAP), whole),
            pl.BlockSpec((CAP, HID), whole),
            pl.BlockSpec((CAP, HID), whole),
        ],
        out_specs=(
            pl.BlockSpec((none, WIDE, HID), lambda i: (0, i, 0)),
            pl.BlockSpec((none, WIDE, HID), lambda i: (0, i, 0)),
            pl.BlockSpec((none, HID, WIDE), lambda i: (0, 0, i)),
        ),
        compiler_params=pltpu.CompilerParams(vmem_limit_bytes=VMEM_BYTES),
        name="weight_grads",
    )(rows_t, scaled, hidden_t, ggp, gup)
    return tok, score, grad_gate, grad_up, grad_down


def solution(mesh):
    in_specs = (
        P("seq", "exp"),
        P("seq", "exp"),
        P(),
        P("seq", None),
        P("seq", None, "exp"),
        P("seq", None, "exp"),
        P("seq", "exp", None),
    )
    out_specs = (
        P("seq", "exp"),
        P("seq", None),
        P("seq", None, "exp"),
        P("seq", None, "exp"),
        P("seq", "exp", None),
    )
    return jax.shard_map(shards, mesh=mesh, in_specs=in_specs, out_specs=out_specs, check_vma=False)
```

time: 172 us -> 85 us (0.49)
  Pallas kernels: 0 us -> 82.6 us
  waiting for transfers between devices: 76.1 us -> 0 us
  matrix products: 46.7 us -> 0 us
  starting transfers between devices: 15.4 us -> 0 us
  blocking collectives: 15.1 us -> 0 us
  between operations: 13.8 us -> 0.66 us
  other arithmetic: 3.1 us -> 0 us
    pallas_call x0 -> x2, Pallas kernels: none -> 82.6 us  [the longest x1 72.1 us: shards(): pl.pallas_call(layer_kernel, out_shape=(shape((CAP, PART), BF16), shape((...]
    dot_general x12 -> x0, matrix products: 46.7 us -> none  [dot(): lax.dot_general(a, b, (((ca,), (cb,)), ((), ())), preferred_element_type=...]
    all_gather x2 -> x0, waiting for transfers between devices: 43.7 us -> none  [the longest x1 23.5 us: shards(): rows = lax.all_gather(mine[:, :part], 'exp', axis=1, tiled=True)]
    all_to_all x2 -> x0, waiting for transfers between devices: 21 us -> none  [the longest x1 16.6 us: shards(): recv = lax.all_to_all(out, 'seq', split_axis=0, concat_axis=0, tiled=True)]
    psum x1 -> x0, blocking collectives: 15.1 us -> none  [shards(): grad_scores = lax.psum(score_part, 'exp')]
    all_to_all x2 -> x0, starting transfers between devices: 15.1 us -> none  [the longest x1 8.13 us: shards(): recv = lax.all_to_all(out, 'seq', split_axis=0, concat_axis=0, tiled=True)]
    reduce_scatter x1 -> x0, waiting for transfers between devices: 10.6 us -> none  [shards(): lax.psum_scatter(partial_value, 'exp', scatter_dimension=1, tiled=True)]
  transfers between devices with their start and end apart: 5 -> 0, of which waited for: 5 -> 0; matrix products, arithmetic and copies ran while one was open for 15% -> 0% of each run, Pallas kernels for 0% -> 0%
where the time goes in v2:
time: 85 us; the launch traced here: 84.5 us
  Pallas kernels  82.6 us (97%)
  local copies, waits for them, and re-layouts  1.29 us (2%)
    pallas_call x1, Pallas kernels, shards(): pl.pallas_call(layer_kernel, out_shape=(shape((CAP, PART), BF16), shape((...  72.1 us
    pallas_call x1, Pallas kernels, shards(): pl.pallas_call(weight_kernel, grid=(CHIPS,), out_shape=(shape((1, CHIPS *...  10.5 us

profile of v2, /device:TPU:0, one launch (start us, length us, event | category | flops | bytes accessed | tf_op | source)
XLA Modules:
  0.0 84.5 jit_solution(8398929264712126183)
XLA Ops:
  0.6 72.1 %layer.1 = (bf16[512,256]{1,0:T(8,128)(2,1)}, f32[1,512]{1,0:T(1,128)}, bf16[4,512,512]{2,1,0:T(8,128)(2,1)}, bf16[4,512,512]{2,1,0:T(8,128)(2,1)}, bf16[1024,51...) custom-call(bf16[512,256]{1,0:T(8,128)(2,1)} %tokens.1, bf16[512,256]{1,0:T(8,128)(2,1)} %grads_in.1, ...), custom_call_target="tpu_custom_call" | custom-call | tf_op jit(solution)/shard_map/layer/pallas_call | solution.py:452
  72.7 0.0 copy-start
  72.7 0.0 copy-start.1
  72.7 10.5 %weight_grads.1 = (bf16[1,2048,1024]{2,1,0:T(8,128)(2,1)}, bf16[1,2048,1024]{2,1,0:T(8,128)(2,1)}, bf16[1,1024,2048]{2,1,0:T(8,128)(2,1)}) custom-call(bf16[4,512,512]{2,1,0:T(8,128)(2,1)} %get-tuple-element.17.rows_t, bf16[4,512,512]{2,1,0:T(8,128)(2,1)} %get-tuple-element.18.scaled, bf16[1024,512]{1,0:T(8,128)(2,1)} %get-tuple-element.19.hidden_t, ...), custom_call_target="tpu_custom_call" | custom-call | tf_op jit(solution)/shard_map/weight_grads/pallas_call | solution.py:524
  83.3 0.0 copy-done
  83.3 0.7 copy.14
  84.0 0.0 copy-done.1
  84.0 0.6 copy.15
Async XLA Ops:
  72.7 10.6 %copy-start = (bf16[512,256]{1,0:T(8,128)(2,1)S(1)}, bf16[512,256]{1,0:T(8,128)(2,1)}, u32[]{:S(2)}) copy-start(bf16[512,256]{1,0:T(8,128)(2,1)} %get-tuple-element.30) | copy-start | bytes 786436
  72.7 11.3 %copy-start.1 = (f32[1,512]{1,0:T(1,128)S(1)}, f32[1,512]{1,0:T(1,128)}, u32[]{:S(2)}) copy-start(f32[1,512]{1,0:T(1,128)} %get-tuple-element.31) | copy-start | bytes 6148

commit v3 on v2

v3 whole, which is shorter than its diff:
```python
import functools

import jax
import jax.numpy as jnp
from jax import lax
from jax.experimental import pallas as pl
from jax.experimental.pallas import tpu as pltpu
from jax.sharding import PartitionSpec as P

MESH = pl.DeviceIdType.MESH
BF16 = jnp.bfloat16
F32 = jnp.float32

OWNERS = 16
MOST = 64
CAP = 512
PART = 256
CHIPS = 4
WIDE = 512
HID = 1024
LANES = 128
VMEM_BYTES = 50 * 1024 * 1024


def dot(a, b):
    return jnp.dot(a, b, preferred_element_type=F32)


def dot_t(a, b):
    return lax.dot_general(a, b, (((1,), (1,)), ((), ())), preferred_element_type=F32)


def iota(shape, axis):
    return lax.broadcasted_iota(jnp.int32, shape, axis)


def part_of(c):
    return pl.ds(pl.multiple_of(c * PART, PART), PART)


def layer_kernel(
    tokens, grads_in, chosen, scores, gate_hbm, up_hbm, down_hbm,
    tok_out, score_out, grad_gate, grad_up, grad_down,
    gate_v, up_v, down_v, full, gate_acc, up_acc, back_acc, hidden, hidden_t, ggp, gup,
    rows_t, send_m, send_t, pick_m, pick_t, out_x, in_x, out_r, in_r, sib_out, sib_in,
    rel_out, rel_in, dir_out, dir_in, fin_out, fin_in, score_buf, gain_col,
    w_sem, x_send, x_recv, g_send, g_recv, s_send, s_recv, c_send, c_recv, r_send, r_recv,
    q_send, q_recv,
):
    seq = lax.axis_index("seq")
    ex = lax.axis_index("exp")
    zz, yy = seq // 4, lax.rem(seq, 4)
    x, c = ex // 2, lax.rem(ex, 2)
    right, left, opp = lax.rem(x + 1, 4), lax.rem(x + 3, 4), lax.rem(x + 2, 4)
    oc = 1 - c

    def seq_peer(k):
        dz, dy = k // 4, lax.rem(k, 4)
        return lax.rem(zz + dz, 4) * 4 + lax.rem(yy + dy, 4)

    def each_peer(step):
        def body(k, carry):
            step(seq_peer(k))
            return carry

        lax.fori_loop(1, OWNERS, body, 0)

    def each_part(step):
        def body(k, carry):
            step(lax.rem(ex + k, 8))
            return carry

        lax.fori_loop(1, 8, body, 0)

    weight_copies = [
        pltpu.make_async_copy(gate_hbm, gate_v, w_sem.at[0]),
        pltpu.make_async_copy(up_hbm, up_v, w_sem.at[1]),
    ] + [
        pltpu.make_async_copy(down_hbm.at[0, :, pl.ds(i * WIDE, WIDE)], down_v.at[i], w_sem.at[2 + i])
        for i in range(CHIPS)
    ]

    barrier = pltpu.get_barrier_semaphore()

    def greet(s, e):
        pl.semaphore_signal(barrier, inc=1, device_id=(s, e), device_id_type=MESH)

    each_peer(lambda peer: greet(peer, ex))
    each_part(lambda peer: greet(seq, peer))
    for copy in weight_copies:
        copy.start()

    lower = seq * CAP
    table = chosen[...]
    begins = jnp.sum((table < lower).astype(jnp.int32), axis=1, keepdims=True)
    mine = jnp.logical_and(table >= lower, table < lower + CAP)
    slots = jnp.where(mine, iota((OWNERS, CAP), 1) - begins, -1)
    local = table - lower
    sub = iota((MOST, CAP), 0)
    lanes = iota((MOST, CAP), 1)
    for e in range(OWNERS):
        hit = slots[e : e + 1, :] == sub
        token = jnp.sum(jnp.where(hit, local[e : e + 1, :] + 1, 0), axis=1, keepdims=True) - 1
        send_m[e * MOST : (e + 1) * MOST, :] = jnp.where(token == lanes, 1.0, 0.0).astype(BF16)

    def slot(owner):
        return pl.ds(pl.multiple_of(owner * MOST, MOST), MOST)

    def x_copy(ch, peer, place):
        return pltpu.make_async_remote_copy(
            src_ref=out_x.at[ch, slot(peer), :],
            dst_ref=in_x.at[ch, slot(place), :],
            send_sem=x_send.at[ch, peer],
            recv_sem=x_recv.at[ch, place],
            device_id=(peer, ex),
            device_id_type=MESH,
        )

    def pack(a, source):
        block = dot(send_m[...], source[...]).astype(BF16)
        out_x[2 * a] = block[:, 0:LANES]
        out_x[2 * a + 1] = block[:, LANES:PART]

    def x_start(ch):
        each_peer(lambda peer: x_copy(ch, peer, seq).start())
        in_x[ch, slot(seq), :] = out_x[ch, slot(seq), :]

    pack(0, tokens)
    pl.semaphore_wait(barrier, OWNERS - 1 + 7)
    x_start(0)
    x_start(1)
    pack(1, grads_in)
    x_start(2)
    x_start(3)

    picked = chosen[pl.ds(seq, 1), :]
    owner_low = iota((OWNERS, CAP), 0) * CAP
    wide = jnp.broadcast_to(picked, (OWNERS, CAP))
    firsts = jnp.sum((wide < owner_low).astype(jnp.int32), axis=1, keepdims=True)
    inside = jnp.logical_and(wide >= owner_low, wide < owner_low + CAP)
    places = jnp.where(inside, iota((OWNERS, CAP), 1) - firsts, -1)
    for g in range(OWNERS // 2):
        block = jnp.concatenate(
            [jnp.where(places[o : o + 1, :] == sub, 1.0, 0.0) for o in (2 * g, 2 * g + 1)], axis=0
        )
        here = slice(g * 2 * MOST, (g + 1) * 2 * MOST)
        pick_t[here, :] = block.astype(BF16)
        pick_m[:, here] = block.T.astype(BF16)
    gain_col[...] = jnp.broadcast_to(scores[...], (128, CAP)).T

    def region(ch, xx, cc):
        a, f = ch // 2, ch % 2
        return full.at[a, xx, :, pl.ds(pl.multiple_of(cc * PART + f * LANES, LANES), LANES)]

    def g_copy(ch, k):
        f = ch % 2
        view, target = {
            0: (region(ch, x, c), (x, oc)),
            1: (region(ch, x, c), (right, c)),
            2: (region(ch, x, c), (left, c)),
            3: (region(ch, left, c), (x, oc)),
            4: (region(ch, right, c), (x, oc)),
            5: (region(ch, left, c), (right, c)) if f == 0 else (region(ch, right, c), (left, c)),
            6: (region(ch, opp, c), (x, oc)),
        }[k]
        return pltpu.make_async_remote_copy(
            src_ref=view, dst_ref=view, send_sem=g_send.at[ch, k], recv_sem=g_recv.at[ch, k],
            device_id=(seq, target[0] * 2 + target[1]), device_id_type=MESH,
        )

    def g_wait(ch, k):
        g_copy(ch, k).wait_recv()

    def g_start(ch, k):
        g_copy(ch, k).start()

    def compact(ch):
        each_peer(lambda peer: x_copy(ch, peer, peer).wait_recv())
        a, f = ch // 2, ch % 2
        cols = pl.ds(pl.multiple_of(c * PART + f * LANES, LANES), LANES)
        full[a, x, :, cols] = dot(pick_m[...], in_x[ch]).astype(BF16)
        for k in (1, 2, 0) if f == 0 else (2, 1, 0):
            g_start(ch, k)

    def relay(ch):
        for k in (1, 2) if ch % 2 == 0 else (2, 1):
            g_wait(ch, k)
            if k == 1 + ch % 2:
                g_start(ch, 5)
            g_start(ch, 2 + k)

    def relay_opp(ch):
        g_wait(ch, 5)
        g_start(ch, 6)

    def gate_up(xx, first):
        def body(n, carry):
            cols = pl.ds(pl.multiple_of(n * WIDE, WIDE), WIDE)
            for acc, w in ((gate_acc, gate_v), (up_acc, up_v)):
                term = dot(full[0, xx], w[xx, :, cols])
                acc[:, cols] = term if first else acc[:, cols] + term
            return carry

        lax.fori_loop(0, HID // WIDE, body, 0)

    def flip_rows(xx):
        rows_t[xx] = full[0, xx].T

    def back(xx, first):
        def body(n, carry):
            cols = pl.ds(pl.multiple_of(n * WIDE, WIDE), WIDE)
            term = dot_t(full[1, xx], down_v[xx, cols, :])
            back_acc[:, cols] = term if first else back_acc[:, cols] + term
            return carry

        lax.fori_loop(0, HID // WIDE, body, 0)

    compact(0)
    compact(1)
    relay(0)
    compact(2)
    relay(1)
    compact(3)
    for copy in weight_copies:
        copy.wait()
    g_wait(0, 0)
    g_wait(1, 0)
    gate_up(x, True)
    relay(2)
    relay_opp(0)
    relay_opp(1)
    g_wait(0, 3)
    g_wait(1, 3)
    gate_up(left, False)
    relay(3)
    g_wait(0, 4)
    g_wait(1, 4)
    gate_up(right, False)
    g_wait(0, 6)
    g_wait(1, 6)
    gate_up(opp, False)
    relay_opp(2)

    def activate(i, carry):
        rows = pl.ds(pl.multiple_of(i * 16, 16), 16)
        pre, up = gate_acc[rows, :], up_acc[rows, :]
        gain = gain_col[rows, 0:1]
        sigma = jax.nn.sigmoid(pre)
        silu = pre * sigma
        hidden[rows, :] = (silu * up).astype(BF16)
        gate_acc[rows, :] = gain * up * sigma * (1.0 + pre * (1.0 - sigma))
        up_acc[rows, :] = gain * silu
        return carry

    lax.fori_loop(0, CAP // 16, activate, 0)
    g_wait(2, 0)
    g_wait(3, 0)
    back(x, True)
    g_wait(2, 3)
    g_wait(3, 3)
    back(left, False)
    g_wait(2, 4)
    g_wait(3, 4)
    back(right, False)
    relay_opp(3)
    flip_rows(x)
    flip_rows(left)
    g_wait(2, 6)
    g_wait(3, 6)
    back(opp, False)

    def finish(i, carry):
        rows = pl.ds(pl.multiple_of(i * 16, 16), 16)
        bh = back_acc[rows, :]
        ggp[rows, :] = (bh * gate_acc[rows, :]).astype(BF16)
        gup[rows, :] = (bh * up_acc[rows, :]).astype(BF16)
        return carry

    lax.fori_loop(0, CAP // 16, finish, 0)

    def contrib(xx, cc):
        feats = part_of(cc)
        return dot_t(ggp[...], gate_v[xx, feats, :]) + dot_t(gup[...], up_v[xx, feats, :])

    order = (opp, left, right, x)

    def s_copy(k):
        return pltpu.make_async_remote_copy(
            src_ref=sib_out.at[k], dst_ref=sib_in.at[k], send_sem=s_send.at[k], recv_sem=s_recv.at[k],
            device_id=(seq, x * 2 + oc), device_id_type=MESH,
        )

    def r_copy(k):
        src, dst, target = (
            (rel_out.at[0], rel_in.at[0], right),
            (rel_out.at[1], rel_in.at[1], left),
            (dir_out.at[0], dir_in.at[0], left),
            (dir_out.at[1], dir_in.at[1], right),
            (fin_out.at[0], fin_in.at[0], right),
            (fin_out.at[1], fin_in.at[1], left),
        )[k]
        return pltpu.make_async_remote_copy(
            src_ref=src, dst_ref=dst, send_sem=r_send.at[k], recv_sem=r_recv.at[k],
            device_id=(seq, target * 2 + c), device_id_type=MESH,
        )

    def for_sibling(k):
        sib_out[k] = contrib(order[k], oc).astype(BF16)
        s_copy(k).start()

    def sums(k, f):
        return gate_acc[:, k * PART + f * LANES : k * PART + (f + 1) * LANES]

    def for_chip(k):
        gate_acc[:, k * PART : (k + 1) * PART] = contrib(order[k], c)

    def add_sibling(k):
        s_copy(k).wait_recv()
        here = slice(k * PART, (k + 1) * PART)
        gate_acc[:, here] = gate_acc[:, here] + sib_in[k].astype(F32)

    for_sibling(0)
    for_sibling(1)
    for_chip(0)
    add_sibling(0)
    rel_out[0] = sums(0, 0).astype(BF16)
    r_copy(0).start()
    rel_out[1] = sums(0, 1).astype(BF16)
    r_copy(1).start()
    for_sibling(2)
    for_chip(1)
    add_sibling(1)
    dir_out[0] = sums(1, 0).astype(BF16)
    r_copy(2).start()
    for_chip(2)
    add_sibling(2)
    dir_out[1] = sums(2, 1).astype(BF16)
    r_copy(3).start()
    for_sibling(3)

    def score_rows(i, carry):
        rows = pl.ds(pl.multiple_of(i * 16, 16), 16)
        prod = hidden[rows, :].astype(F32) * back_acc[rows, :]
        part = prod[:, 0:128]
        for j in range(1, HID // 128):
            part = part + prod[:, j * 128 : (j + 1) * 128]
        back_acc[rows, 0:128] = part
        return carry

    def q_copy(peer, place):
        return pltpu.make_async_remote_copy(
            src_ref=score_buf.at[ex], dst_ref=score_buf.at[place], send_sem=q_send.at[peer], recv_sem=q_recv.at[place],
            device_id=(seq, peer), device_id_type=MESH,
        )

    lax.fori_loop(0, CAP // 16, score_rows, 0)
    r_copy(0).wait_recv()
    fin_out[0] = (sums(2, 0) + rel_in[0].astype(F32)).astype(BF16)
    r_copy(4).start()
    r_copy(1).wait_recv()
    fin_out[1] = (sums(1, 1) + rel_in[1].astype(F32)).astype(BF16)
    r_copy(5).start()
    for_chip(3)
    score_part = jnp.sum(back_acc[:, 0:128].T, axis=0, keepdims=True)
    score_buf[ex] = jnp.broadcast_to(score_part, (8, CAP))
    each_part(lambda peer: q_copy(peer, ex).start())

    def weight_rows(xx):
        def body(n, carry):
            cols = pl.ds(pl.multiple_of(n * WIDE, WIDE), WIDE)
            here = pl.ds(pl.multiple_of(xx * WIDE, WIDE), WIDE)
            grad_gate[here, cols] = dot(rows_t[xx], ggp[:, cols]).astype(BF16)
            grad_up[here, cols] = dot(rows_t[xx], gup[:, cols]).astype(BF16)
            return carry

        lax.fori_loop(0, HID // WIDE, body, 0)

    def weight_down(i):
        full[1, i] = (gain_col[:, 0:1] * full[1, i].astype(F32)).astype(BF16)

        def body(n, carry):
            here = pl.ds(pl.multiple_of(n * WIDE, WIDE), WIDE)
            grad_down[here, i * WIDE : (i + 1) * WIDE] = dot(hidden_t[here, :], full[1, i]).astype(BF16)
            return carry

        lax.fori_loop(0, HID // WIDE, body, 0)

    def c_copy(f, peer, place):
        return pltpu.make_async_remote_copy(
            src_ref=out_r.at[f, slot(peer), :],
            dst_ref=in_r.at[f, slot(place), :],
            send_sem=c_send.at[f, peer],
            recv_sem=c_recv.at[f, place],
            device_id=(peer, ex),
            device_id_type=MESH,
        )

    def give_back(f):
        r_copy(2 + f).wait_recv()
        r_copy(4 + f).wait_recv()
        summed = (sums(3, f) + fin_in[f].astype(F32) + dir_in[f].astype(F32)).astype(BF16)
        out_r[f] = dot(pick_t[...], summed).astype(BF16)
        each_peer(lambda peer: c_copy(f, peer, seq).start())
        in_r[f, slot(seq), :] = out_r[f, slot(seq), :]

    weight_rows(x)
    add_sibling(3)
    weight_rows(left)
    flip_rows(right)
    give_back(0)
    weight_rows(right)
    give_back(1)
    flip_rows(opp)
    weight_rows(opp)
    hidden_t[...] = hidden[...].T
    for ch in (2, 3):
        for k in range(7):
            g_copy(ch, k).wait_send()
    for i in range(CHIPS):
        weight_down(i)
    for g in range(OWNERS // 2):
        here = slice(g * 2 * MOST, (g + 1) * 2 * MOST)
        send_t[:, here] = send_m[here, :].astype(F32).T.astype(BF16)

    each_part(lambda peer: q_copy(peer, peer).wait_recv())
    total = score_buf[0, 0:1, :]
    for i in range(1, 8):
        total = total + score_buf[i, 0:1, :]
    score_out[...] = total

    for f in range(2):
        each_peer(lambda peer: c_copy(f, peer, peer).wait_recv())
        tok_out[:, f * LANES : (f + 1) * LANES] = dot(send_t[...], in_r[f]).astype(BF16)

    def sent(peer):
        for ch in range(4):
            x_copy(ch, peer, seq).wait_send()
        for f in range(2):
            c_copy(f, peer, seq).wait_send()

    each_peer(sent)
    each_part(lambda peer: q_copy(peer, ex).wait_send())
    for k in range(7):
        g_copy(0, k).wait_send()
        g_copy(1, k).wait_send()
    for k in range(4):
        s_copy(k).wait_send()
    for k in range(6):
        r_copy(k).wait_send()


def store_kernel(*refs):
    count = (len(refs) - 1) // 2
    sems = refs[-1]
    copies = []
    for src, dst in zip(refs[:count], refs[count : 2 * count]):
        cuts = 4 if src.shape[0] >= 1024 else 1
        rows = src.shape[0] // cuts
        for i in range(cuts):
            here = pl.ds(i * rows, rows)
            copies.append(pltpu.make_async_copy(src.at[here, :], dst.at[here, :], sems.at[len(copies)]))
    for copy in copies:
        copy.start()
    for copy in copies:
        copy.wait()


def shards(tokens, grad_out, chosen, scores, gate_weight, up_weight, down_weight):
    vmem = pl.BlockSpec(memory_space=pltpu.VMEM)
    anyw = pl.BlockSpec(memory_space=pl.ANY)
    shape = jax.ShapeDtypeStruct
    dma = pltpu.SemaphoreType.DMA
    results = (
        ((CAP, PART), BF16),
        ((1, CAP), F32),
        ((CHIPS * WIDE, HID), BF16),
        ((CHIPS * WIDE, HID), BF16),
        ((HID, CHIPS * WIDE), BF16),
    )
    kept = pl.pallas_call(
        layer_kernel,
        out_shape=tuple(pltpu.VMEM(*r) for r in results),
        in_specs=[vmem] * 4 + [anyw] * 3,
        out_specs=(vmem,) * 5,
        scratch_shapes=[
            pltpu.VMEM((CHIPS, WIDE, HID), BF16),
            pltpu.VMEM((CHIPS, WIDE, HID), BF16),
            pltpu.VMEM((CHIPS, HID, WIDE), BF16),
            pltpu.VMEM((2, CHIPS, CAP, WIDE), BF16),
            pltpu.VMEM((CAP, HID), F32),
            pltpu.VMEM((CAP, HID), F32),
            pltpu.VMEM((CAP, HID), F32),
            pltpu.VMEM((CAP, HID), BF16),
            pltpu.VMEM((HID, CAP), BF16),
            pltpu.VMEM((CAP, HID), BF16),
            pltpu.VMEM((CAP, HID), BF16),
            pltpu.VMEM((CHIPS, WIDE, CAP), BF16),
            pltpu.VMEM((OWNERS * MOST, CAP), BF16),
            pltpu.VMEM((CAP, OWNERS * MOST), BF16),
            pltpu.VMEM((CAP, OWNERS * MOST), BF16),
            pltpu.VMEM((OWNERS * MOST, CAP), BF16),
            pltpu.VMEM((4, OWNERS * MOST, LANES), BF16),
            pltpu.VMEM((4, OWNERS * MOST, LANES), BF16),
            pltpu.VMEM((2, OWNERS * MOST, LANES), BF16),
            pltpu.VMEM((2, OWNERS * MOST, LANES), BF16),
            pltpu.VMEM((CHIPS, CAP, PART), BF16),
            pltpu.VMEM((CHIPS, CAP, PART), BF16),
        ]
        + [pltpu.VMEM((2, CAP, LANES), BF16)] * 6
        + [
            pltpu.VMEM((8, 8, CAP), F32),
            pltpu.VMEM((CAP, 128), F32),
            dma((2 + CHIPS,)),
            dma((4, OWNERS)),
            dma((4, OWNERS)),
            dma((4, 7)),
            dma((4, 7)),
            dma((4,)),
            dma((4,)),
            dma((2, OWNERS)),
            dma((2, OWNERS)),
            dma((6,)),
            dma((6,)),
            dma((8,)),
            dma((8,)),
        ],
        compiler_params=pltpu.CompilerParams(
            collective_id=0, has_side_effects=True, vmem_limit_bytes=VMEM_BYTES
        ),
        name="layer",
    )(
        tokens,
        grad_out,
        chosen,
        scores,
        gate_weight.reshape(CHIPS, WIDE, HID),
        up_weight.reshape(CHIPS, WIDE, HID),
        down_weight,
    )
    tok, score, grad_gate, grad_up, grad_down = pl.pallas_call(
        store_kernel,
        out_shape=tuple(shape(*r) for r in results),
        in_specs=[vmem] * 5,
        out_specs=(anyw,) * 5,
        scratch_shapes=[dma((16,))],
        compiler_params=pltpu.CompilerParams(vmem_limit_bytes=1024 * 1024),
        name="store",
    )(*[pltpu.with_memory_space_constraint(k, pltpu.VMEM) for k in kept])
    return tok, score, grad_gate[None], grad_up[None], grad_down[None]


def solution(mesh):
    in_specs = (
        P("seq", "exp"),
        P("seq", "exp"),
        P(),
        P("seq", None),
        P("seq", None, "exp"),
        P("seq", None, "exp"),
        P("seq", "exp", None),
    )
    out_specs = (
        P("seq", "exp"),
        P("seq", None),
        P("seq", None, "exp"),
        P("seq", None, "exp"),
        P("seq", "exp", None),
    )
    return jax.shard_map(shards, mesh=mesh, in_specs=in_specs, out_specs=out_specs, check_vma=False)
```

time: 85 us -> 79.8 us (0.939); the launches traced: 84.5 us -> 78.2 us
  Pallas kernels: 82.6 us -> 77.4 us
  local copies, waits for them, and re-layouts: 1.29 us -> 0 us
    pallas_call x2, Pallas kernels: 82.6 us -> 77.4 us  [the longest x1 72.6 us: shards(): pl.pallas_call(layer_kernel, out_shape=tuple((pltpu.VMEM(*r) for r in res...]
    unnamed x6 -> x0, local copies, waits for them, and re-layouts: 1.29 us -> none
where the time goes in v3:
time: 79.8 us; the launch traced here: 78.2 us
  Pallas kernels  77.4 us (97%)
  between operations  0.8 us (1%)
    pallas_call x1, Pallas kernels, shards(): pl.pallas_call(layer_kernel, out_shape=tuple((pltpu.VMEM(*r) for r in res...  72.6 us
    pallas_call x1, Pallas kernels, shards(): pl.pallas_call(store_kernel, out_shape=tuple((shape(*r) for r in results)...  4.79 us

profile of v3, /device:TPU:0, one launch (start us, length us, event | category | flops | bytes accessed | tf_op | source)
XLA Modules:
  0.0 78.2 jit_solution(15739593678678936876)
XLA Ops:
  0.6 72.6 %layer.1 = (bf16[512,256]{1,0:T(8,128)(2,1)S(1)}, f32[1,512]{1,0:T(1,128)S(1)}, bf16[2048,1024]{1,0:T(8,128)(2,1)S(1)}, bf16[2048,1024]{1,0:T(8,128)(2,1)S(1)}, bf16[1024,2048]{1,0:T(8,128)(2,1)S(1)}) custom-call(bf16[512,256]{1,0:T(8,128)(2,1)} %tokens.1, bf16[512,256]{1,0:T(8,128)(2,1)} %grads_in.1, s32[16,512]{1,0:T(8,128)} %chosen.1, f32[1,512]{1,0:T(1,128)} %scores.1, ...), custom_call_target="tpu_custom_call" | custom-call | tf_op jit(solution)/shard_map/layer/pallas_call | solution.py:480
  73.3 4.8 %store.1 = (bf16[512,256]{1,0:T(8,128)(2,1)}, f32[1,512]{1,0:T(1,128)}, bf16[2048,1024]{1,0:T(8,128)(2,1)}, bf16[2048,1024]{1,0:T(8,128)(2,1)}, bf16[1024,2048]{1,0:T(8,128)(2,1)}) custom-call(bf16[512,256]{1,0:T(8,128)(2,1)S(1)} %get-tuple-element.15.refs_0_, f32[1,512]{1,0:T(1,128)S(1)} %get-tuple-element.16.refs_1_, ...), custom_call_target="tpu_custom_call" | custom-call | tf_op jit(solution)/shard_map/store/pallas_call | solution.py:540

commit v4 on v3

--- a/solution.py
+++ b/solution.py
@@ -19,6 +19,7 @@
 WIDE = 512
 HID = 1024
 LANES = 128
+HALF = CAP // 2
 VMEM_BYTES = 50 * 1024 * 1024
 
 
@@ -40,8 +41,8 @@
 
 def layer_kernel(
     tokens, grads_in, chosen, scores, gate_hbm, up_hbm, down_hbm,
-    tok_out, score_out, grad_gate, grad_up, grad_down,
-    gate_v, up_v, down_v, full, gate_acc, up_acc, back_acc, hidden, hidden_t, ggp, gup,
+    tok_out, score_out, grad_gate, grad_up, hidden_t, scaled,
+    gate_v, up_v, down_v, full, gate_acc, up_acc, back_acc, hidden, ggp, gup,
     rows_t, send_m, send_t, pick_m, pick_t, out_x, in_x, out_r, in_r, sib_out, sib_in,
     rel_out, rel_in, dir_out, dir_in, fin_out, fin_in, score_buf, gain_col,
     w_sem, x_send, x_recv, g_send, g_recv, s_send, s_recv, c_send, c_recv, r_send, r_recv,
@@ -146,6 +147,7 @@
         here = slice(g * 2 * MOST, (g + 1) * 2 * MOST)
         pick_t[here, :] = block.astype(BF16)
         pick_m[:, here] = block.T.astype(BF16)
+        send_t[:, here] = send_m[here, :].astype(F32).T.astype(BF16)
     gain_col[...] = jnp.broadcast_to(scores[...], (128, CAP)).T
 
     def region(ch, xx, cc):
@@ -206,6 +208,9 @@
     def flip_rows(xx):
         rows_t[xx] = full[0, xx].T
 
+    def scale(xx):
+        scaled[xx] = (gain_col[:, 0:1] * full[1, xx].astype(F32)).astype(BF16)
+
     def back(xx, first):
         def body(n, carry):
             cols = pl.ds(pl.multiple_of(n * WIDE, WIDE), WIDE)
@@ -215,31 +220,31 @@
 
         lax.fori_loop(0, HID // WIDE, body, 0)
 
+    def g_wait_both(a, k):
+        g_wait(2 * a, k)
+        g_wait(2 * a + 1, k)
+
     compact(0)
     compact(1)
     relay(0)
+    for copy in weight_copies:
+        copy.wait()
+    g_wait_both(0, 0)
+    gate_up(x, True)
     compact(2)
     relay(1)
     compact(3)
-    for copy in weight_copies:
-        copy.wait()
-    g_wait(0, 0)
-    g_wait(1, 0)
-    gate_up(x, True)
-    relay(2)
+    g_wait_both(0, 3)
+    gate_up(left, False)
+    g_wait_both(0, 4)
+    gate_up(right, False)
     relay_opp(0)
     relay_opp(1)
-    g_wait(0, 3)
-    g_wait(1, 3)
-    gate_up(left, False)
+    relay(2)
+    flip_rows(x)
+    g_wait_both(0, 6)
+    gate_up(opp, False)
     relay(3)
-    g_wait(0, 4)
-    g_wait(1, 4)
-    gate_up(right, False)
-    g_wait(0, 6)
-    g_wait(1, 6)
-    gate_up(opp, False)
-    relay_opp(2)
 
     def activate(i, carry):
         rows = pl.ds(pl.multiple_of(i * 16, 16), 16)
@@ -253,20 +258,19 @@
         return carry
 
     lax.fori_loop(0, CAP // 16, activate, 0)
-    g_wait(2, 0)
-    g_wait(3, 0)
+    g_wait_both(1, 0)
     back(x, True)
-    g_wait(2, 3)
-    g_wait(3, 3)
+    g_wait_both(1, 3)
     back(left, False)
-    g_wait(2, 4)
-    g_wait(3, 4)
+    relay_opp(2)
+    g_wait_both(1, 4)
     back(right, False)
+    flip_rows(left)
+    flip_rows(right)
     relay_opp(3)
-    flip_rows(x)
-    flip_rows(left)
-    g_wait(2, 6)
-    g_wait(3, 6)
+    flip_rows(opp)
+    hidden_t[...] = hidden[...].T
+    g_wait_both(1, 6)
     back(opp, False)
 
     def finish(i, carry):
@@ -290,17 +294,17 @@
             device_id=(seq, x * 2 + oc), device_id_type=MESH,
         )
 
-    def r_copy(k):
+    def r_copy(f, k):
         src, dst, target = (
-            (rel_out.at[0], rel_in.at[0], right),
-            (rel_out.at[1], rel_in.at[1], left),
-            (dir_out.at[0], dir_in.at[0], left),
-            (dir_out.at[1], dir_in.at[1], right),
-            (fin_out.at[0], fin_in.at[0], right),
-            (fin_out.at[1], fin_in.at[1], left),
+            (rel_out.at[f, 0], rel_in.at[f, 0], right),
+            (rel_out.at[f, 1], rel_in.at[f, 1], left),
+            (dir_out.at[f, 0], dir_in.at[f, 0], left),
+            (dir_out.at[f, 1], dir_in.at[f, 1], right),
+            (fin_out.at[f, 0], fin_in.at[f, 0], right),
+            (fin_out.at[f, 1], fin_in.at[f, 1], left),
         )[k]
         return pltpu.make_async_remote_copy(
-            src_ref=src, dst_ref=dst, send_sem=r_send.at[k], recv_sem=r_recv.at[k],
+            src_ref=src, dst_ref=dst, send_sem=r_send.at[f, k], recv_sem=r_recv.at[f, k],
             device_id=(seq, target * 2 + c), device_id_type=MESH,
         )
 
@@ -308,8 +312,9 @@
         sib_out[k] = contrib(order[k], oc).astype(BF16)
         s_copy(k).start()
 
-    def sums(k, f):
-        return gate_acc[:, k * PART + f * LANES : k * PART + (f + 1) * LANES]
+    def sums(k, f, h):
+        cols = k * PART + f * LANES
+        return gate_acc[h * HALF : (h + 1) * HALF, cols : cols + LANES]
 
     def for_chip(k):
         gate_acc[:, k * PART : (k + 1) * PART] = contrib(order[k], c)
@@ -319,23 +324,31 @@
         here = slice(k * PART, (k + 1) * PART)
         gate_acc[:, here] = gate_acc[:, here] + sib_in[k].astype(F32)
 
+    def send_direct(f, h):
+        dir_out[f, h] = sums(1 + h, f, h).astype(BF16)
+        r_copy(f, 2 + h).start()
+
+    def send_final(f):
+        for h in range(2):
+            r_copy(f, h).wait_recv()
+            fin_out[f, h] = (sums(2 - h, f, h) + rel_in[f, h].astype(F32)).astype(BF16)
+            r_copy(f, 4 + h).start()
+
     for_sibling(0)
     for_sibling(1)
     for_chip(0)
     add_sibling(0)
-    rel_out[0] = sums(0, 0).astype(BF16)
-    r_copy(0).start()
-    rel_out[1] = sums(0, 1).astype(BF16)
-    r_copy(1).start()
+    for f in range(2):
+        for h in range(2):
+            rel_out[f, h] = sums(0, f, h).astype(BF16)
+            r_copy(f, h).start()
     for_sibling(2)
     for_chip(1)
     add_sibling(1)
-    dir_out[0] = sums(1, 0).astype(BF16)
-    r_copy(2).start()
+    send_direct(0, 0)
     for_chip(2)
     add_sibling(2)
-    dir_out[1] = sums(2, 1).astype(BF16)
-    r_copy(3).start()
+    send_direct(0, 1)
     for_sibling(3)
 
     def score_rows(i, carry):
@@ -353,16 +366,14 @@
             device_id=(seq, peer), device_id_type=MESH,
         )
 
+    send_final(0)
+    send_direct(1, 0)
+    send_direct(1, 1)
+    for_chip(3)
     lax.fori_loop(0, CAP // 16, score_rows, 0)
-    r_copy(0).wait_recv()
-    fin_out[0] = (sums(2, 0) + rel_in[0].astype(F32)).astype(BF16)
-    r_copy(4).start()
-    r_copy(1).wait_recv()
-    fin_out[1] = (sums(1, 1) + rel_in[1].astype(F32)).astype(BF16)
-    r_copy(5).start()
-    for_chip(3)
+    send_final(1)
     score_part = jnp.sum(back_acc[:, 0:128].T, axis=0, keepdims=True)
-    score_buf[ex] = jnp.broadcast_to(score_part, (8, CAP))
+    score_buf[ex] = score_part
     each_part(lambda peer: q_copy(peer, ex).start())
 
     def weight_rows(xx):
@@ -371,16 +382,6 @@
             here = pl.ds(pl.multiple_of(xx * WIDE, WIDE), WIDE)
             grad_gate[here, cols] = dot(rows_t[xx], ggp[:, cols]).astype(BF16)
             grad_up[here, cols] = dot(rows_t[xx], gup[:, cols]).astype(BF16)
-            return carry
-
-        lax.fori_loop(0, HID // WIDE, body, 0)
-
-    def weight_down(i):
-        full[1, i] = (gain_col[:, 0:1] * full[1, i].astype(F32)).astype(BF16)
-
-        def body(n, carry):
-            here = pl.ds(pl.multiple_of(n * WIDE, WIDE), WIDE)
-            grad_down[here, i * WIDE : (i + 1) * WIDE] = dot(hidden_t[here, :], full[1, i]).astype(BF16)
             return carry
 
         lax.fori_loop(0, HID // WIDE, body, 0)
@@ -396,36 +397,29 @@
         )
 
     def give_back(f):
-        r_copy(2 + f).wait_recv()
-        r_copy(4 + f).wait_recv()
-        summed = (sums(3, f) + fin_in[f].astype(F32) + dir_in[f].astype(F32)).astype(BF16)
-        out_r[f] = dot(pick_t[...], summed).astype(BF16)
+        for k in (2, 3, 4, 5):
+            r_copy(f, k).wait_recv()
+        halves = [
+            (sums(3, f, h) + fin_in[f, h].astype(F32) + dir_in[f, h].astype(F32)).astype(BF16) for h in range(2)
+        ]
+        out_r[f] = dot(pick_t[...], jnp.concatenate(halves, axis=0)).astype(BF16)
         each_peer(lambda peer: c_copy(f, peer, seq).start())
         in_r[f, slot(seq), :] = out_r[f, slot(seq), :]
 
+    add_sibling(3)
     weight_rows(x)
-    add_sibling(3)
+    give_back(0)
     weight_rows(left)
-    flip_rows(right)
-    give_back(0)
+    give_back(1)
     weight_rows(right)
-    give_back(1)
-    flip_rows(opp)
     weight_rows(opp)
-    hidden_t[...] = hidden[...].T
-    for ch in (2, 3):
-        for k in range(7):
-            g_copy(ch, k).wait_send()
-    for i in range(CHIPS):
-        weight_down(i)
-    for g in range(OWNERS // 2):
-        here = slice(g * 2 * MOST, (g + 1) * 2 * MOST)
-        send_t[:, here] = send_m[here, :].astype(F32).T.astype(BF16)
+    for xx in range(CHIPS):
+        scale(xx)
 
     each_part(lambda peer: q_copy(peer, peer).wait_recv())
-    total = score_buf[0, 0:1, :]
+    total = score_buf[0]
     for i in range(1, 8):
-        total = total + score_buf[i, 0:1, :]
+        total = total + score_buf[i]
     score_out[...] = total
 
     for f in range(2):
@@ -440,27 +434,40 @@
 
     each_peer(sent)
     each_part(lambda peer: q_copy(peer, ex).wait_send())
-    for k in range(7):
-        g_copy(0, k).wait_send()
-        g_copy(1, k).wait_send()
+    for ch in range(4):
+        for k in range(7):
+            g_copy(ch, k).wait_send()
     for k in range(4):
         s_copy(k).wait_send()
-    for k in range(6):
-        r_copy(k).wait_send()
-
-
-def store_kernel(*refs):
-    count = (len(refs) - 1) // 2
-    sems = refs[-1]
-    copies = []
-    for src, dst in zip(refs[:count], refs[count : 2 * count]):
-        cuts = 4 if src.shape[0] >= 1024 else 1
-        rows = src.shape[0] // cuts
-        for i in range(cuts):
-            here = pl.ds(i * rows, rows)
+    for f in range(2):
+        for k in range(6):
+            r_copy(f, k).wait_send()
+
+
+def store_kernel(
+    tok, score, grad_gate, grad_up, hidden_t, scaled, tok_hbm, score_hbm, gate_hbm, up_hbm, down_hbm, stage, sems
+):
+    copies = [
+        pltpu.make_async_copy(tok, tok_hbm, sems.at[0]),
+        pltpu.make_async_copy(score, score_hbm, sems.at[1]),
+    ]
+    for src, dst in ((grad_gate, gate_hbm), (grad_up, up_hbm)):
+        for i in range(CHIPS):
+            here = pl.ds(i * WIDE, WIDE)
             copies.append(pltpu.make_async_copy(src.at[here, :], dst.at[here, :], sems.at[len(copies)]))
     for copy in copies:
         copy.start()
+    for i in range(CHIPS):
+
+        def body(n, carry):
+            here = pl.ds(pl.multiple_of(n * WIDE, WIDE), WIDE)
+            stage[i, here, :] = dot(hidden_t[here, :], scaled[i]).astype(BF16)
+            return carry
+
+        lax.fori_loop(0, HID // WIDE, body, 0)
+        last = pltpu.make_async_copy(stage.at[i], down_hbm.at[:, pl.ds(i * WIDE, WIDE)], sems.at[len(copies)])
+        last.start()
+        copies.append(last)
     for copy in copies:
         copy.wait()
 
@@ -470,18 +477,14 @@
     anyw = pl.BlockSpec(memory_space=pl.ANY)
     shape = jax.ShapeDtypeStruct
     dma = pltpu.SemaphoreType.DMA
-    results = (
-        ((CAP, PART), BF16),
-        ((1, CAP), F32),
-        ((CHIPS * WIDE, HID), BF16),
-        ((CHIPS * WIDE, HID), BF16),
-        ((HID, CHIPS * WIDE), BF16),
-    )
+    first = (((CAP, PART), BF16), ((1, CAP), F32), ((CHIPS * WIDE, HID), BF16), ((CHIPS * WIDE, HID), BF16))
+    left_over = (((HID, CAP), BF16), ((CHIPS, CAP, WIDE), BF16))
+    results = first + (((HID, CHIPS * WIDE), BF16),)
     kept = pl.pallas_call(
         layer_kernel,
-        out_shape=tuple(pltpu.VMEM(*r) for r in results),
+        out_shape=tuple(pltpu.VMEM(*r) for r in first + left_over),
         in_specs=[vmem] * 4 + [anyw] * 3,
-        out_specs=(vmem,) * 5,
+        out_specs=(vmem,) * 6,
         scratch_shapes=[
             pltpu.VMEM((CHIPS, WIDE, HID), BF16),
             pltpu.VMEM((CHIPS, WIDE, HID), BF16),
@@ -491,7 +494,6 @@
             pltpu.VMEM((CAP, HID), F32),
             pltpu.VMEM((CAP, HID), F32),
             pltpu.VMEM((CAP, HID), BF16),
-            pltpu.VMEM((HID, CAP), BF16),
             pltpu.VMEM((CAP, HID), BF16),
             pltpu.VMEM((CAP, HID), BF16),
             pltpu.VMEM((CHIPS, WIDE, CAP), BF16),
@@ -506,9 +508,9 @@
             pltpu.VMEM((CHIPS, CAP, PART), BF16),
             pltpu.VMEM((CHIPS, CAP, PART), BF16),
         ]
-        + [pltpu.VMEM((2, CAP, LANES), BF16)] * 6
+        + [pltpu.VMEM((2, 2, HALF, LANES), BF16)] * 6
         + [
-            pltpu.VMEM((8, 8, CAP), F32),
+            pltpu.VMEM((8, 1, CAP), F32),
             pltpu.VMEM((CAP, 128), F32),
             dma((2 + CHIPS,)),
             dma((4, OWNERS)),
@@ -519,8 +521,8 @@
             dma((4,)),
             dma((2, OWNERS)),
             dma((2, OWNERS)),
-            dma((6,)),
-            dma((6,)),
+            dma((2, 6)),
+            dma((2, 6)),
             dma((8,)),
             dma((8,)),
         ],
@@ -540,10 +542,10 @@
     tok, score, grad_gate, grad_up, grad_down = pl.pallas_call(
         store_kernel,
         out_shape=tuple(shape(*r) for r in results),
-        in_specs=[vmem] * 5,
+        in_specs=[vmem] * 6,
         out_specs=(anyw,) * 5,
-        scratch_shapes=[dma((16,))],
-        compiler_params=pltpu.CompilerParams(vmem_limit_bytes=1024 * 1024),
+        scratch_shapes=[pltpu.VMEM((CHIPS, HID, WIDE), BF16), dma((16,))],
+        compiler_params=pltpu.CompilerParams(vmem_limit_bytes=8 * 1024 * 1024),
         name="store",
     )(*[pltpu.with_memory_space_constraint(k, pltpu.VMEM) for k in kept])
     return tok, score, grad_gate[None], grad_up[None], grad_down[None]

time: 79.8 us -> 74.5 us (0.934); the launches traced: 78.2 us -> 74.4 us
  Pallas kernels: 77.4 us -> 73.6 us
    pallas_call x1, Pallas kernels: 72.6 us -> 68.8 us  [shards(): pl.pallas_call(layer_kernel, out_shape=tuple((pltpu.VMEM(*r) for r in fir...]
where the time goes in v4:
time: 74.5 us; the launch traced here: 74.4 us
  Pallas kernels  73.6 us (99%)
  between operations  0.8 us (1%)
    pallas_call x1, Pallas kernels, shards(): pl.pallas_call(layer_kernel, out_shape=tuple((pltpu.VMEM(*r) for r in fir...  68.8 us
    pallas_call x1, Pallas kernels, shards(): pl.pallas_call(store_kernel, out_shape=tuple((shape(*r) for r in results)...  4.79 us

profile of v4, /device:TPU:0, one launch (start us, length us, event | category | flops | bytes accessed | tf_op | source)
XLA Modules:
  0.0 74.4 jit_solution(18349177219781817868)
XLA Ops:
  0.6 68.8 %layer.1 = (bf16[512,256]{1,0:T(8,128)(2,1)S(1)}, f32[1,512]{1,0:T(1,128)S(1)}, bf16[2048,1024]{1,0:T(8,128)(2,1)S(1)}, bf16[2048,1024]{1,0:T(8,128)(2,1)S(1)}, ...) custom-call(bf16[512,256]{1,0:T(8,128)(2,1)} %tokens.1, bf16[512,256]{1,0:T(8,128)(2,1)} %grads_in.1, ...), custom_call_target="tpu_custom_call" | custom-call | tf_op jit(solution)/shard_map/layer/pallas_call | solution.py:483
  69.5 4.8 %store.1 = (bf16[512,256]{1,0:T(8,128)(2,1)}, f32[1,512]{1,0:T(1,128)}, bf16[2048,1024]{1,0:T(8,128)(2,1)}, bf16[2048,1024]{1,0:T(8,128)(2,1)}, bf16[1024,2048]{1,0:T(8,128)(2,1)}) custom-call(bf16[512,256]{1,0:T(8,128)(2,1)S(1)} %get-tuple-element.16.tok, f32[1,512]{1,0:T(1,128)S(1)} %get-tuple-element.17.score, ...), custom_call_target="tpu_custom_call" | custom-call | tf_op jit(solution)/shard_map/store/pallas_call | solution.py:542

commit v5 on v4

--- a/solution.py
+++ b/solution.py
@@ -130,10 +130,6 @@
     pl.semaphore_wait(barrier, OWNERS - 1 + 7)
     x_start(0)
     x_start(1)
-    pack(1, grads_in)
-    x_start(2)
-    x_start(3)
-
     picked = chosen[pl.ds(seq, 1), :]
     owner_low = iota((OWNERS, CAP), 0) * CAP
     wide = jnp.broadcast_to(picked, (OWNERS, CAP))
@@ -147,8 +143,13 @@
         here = slice(g * 2 * MOST, (g + 1) * 2 * MOST)
         pick_t[here, :] = block.astype(BF16)
         pick_m[:, here] = block.T.astype(BF16)
+    pack(1, grads_in)
+    x_start(2)
+    x_start(3)
+    gain_col[...] = jnp.broadcast_to(scores[...], (128, CAP)).T
+    for g in range(OWNERS // 2):
+        here = slice(g * 2 * MOST, (g + 1) * 2 * MOST)
         send_t[:, here] = send_m[here, :].astype(F32).T.astype(BF16)
-    gain_col[...] = jnp.broadcast_to(scores[...], (128, CAP)).T
 
     def region(ch, xx, cc):
         a, f = ch // 2, ch % 2
@@ -196,14 +197,14 @@
         g_start(ch, 6)
 
     def gate_up(xx, first):
-        def body(n, carry):
-            cols = pl.ds(pl.multiple_of(n * WIDE, WIDE), WIDE)
+        def body(n):
+            cols = slice(n * WIDE, (n + 1) * WIDE)
             for acc, w in ((gate_acc, gate_v), (up_acc, up_v)):
                 term = dot(full[0, xx], w[xx, :, cols])
                 acc[:, cols] = term if first else acc[:, cols] + term
-            return carry
-
-        lax.fori_loop(0, HID // WIDE, body, 0)
+
+        for n in range(HID // WIDE):
+            body(n)
 
     def flip_rows(xx):
         rows_t[xx] = full[0, xx].T
@@ -212,13 +213,13 @@
         scaled[xx] = (gain_col[:, 0:1] * full[1, xx].astype(F32)).astype(BF16)
 
     def back(xx, first):
-        def body(n, carry):
-            cols = pl.ds(pl.multiple_of(n * WIDE, WIDE), WIDE)
+        def body(n):
+            cols = slice(n * WIDE, (n + 1) * WIDE)
             term = dot_t(full[1, xx], down_v[xx, cols, :])
             back_acc[:, cols] = term if first else back_acc[:, cols] + term
-            return carry
-
-        lax.fori_loop(0, HID // WIDE, body, 0)
+
+        for n in range(HID // WIDE):
+            body(n)
 
     def g_wait_both(a, k):
         g_wait(2 * a, k)
@@ -226,11 +227,11 @@
 
     compact(0)
     compact(1)
-    relay(0)
     for copy in weight_copies:
         copy.wait()
     g_wait_both(0, 0)
     gate_up(x, True)
+    relay(0)
     compact(2)
     relay(1)
     compact(3)
@@ -257,7 +258,7 @@
         up_acc[rows, :] = gain * silu
         return carry
 
-    lax.fori_loop(0, CAP // 16, activate, 0)
+    lax.fori_loop(0, CAP // 16, activate, 0, unroll=2)
     g_wait_both(1, 0)
     back(x, True)
     g_wait_both(1, 3)
@@ -280,7 +281,7 @@
         gup[rows, :] = (bh * up_acc[rows, :]).astype(BF16)
         return carry
 
-    lax.fori_loop(0, CAP // 16, finish, 0)
+    lax.fori_loop(0, CAP // 16, finish, 0, unroll=4)
 
     def contrib(xx, cc):
         feats = part_of(cc)
@@ -370,21 +371,21 @@
     send_direct(1, 0)
     send_direct(1, 1)
     for_chip(3)
-    lax.fori_loop(0, CAP // 16, score_rows, 0)
+    lax.fori_loop(0, CAP // 16, score_rows, 0, unroll=2)
     send_final(1)
     score_part = jnp.sum(back_acc[:, 0:128].T, axis=0, keepdims=True)
     score_buf[ex] = score_part
     each_part(lambda peer: q_copy(peer, ex).start())
 
     def weight_rows(xx):
-        def body(n, carry):
-            cols = pl.ds(pl.multiple_of(n * WIDE, WIDE), WIDE)
+        def body(n):
+            cols = slice(n * WIDE, (n + 1) * WIDE)
             here = pl.ds(pl.multiple_of(xx * WIDE, WIDE), WIDE)
             grad_gate[here, cols] = dot(rows_t[xx], ggp[:, cols]).astype(BF16)
             grad_up[here, cols] = dot(rows_t[xx], gup[:, cols]).astype(BF16)
-            return carry
-
-        lax.fori_loop(0, HID // WIDE, body, 0)
+
+        for n in range(HID // WIDE):
+            body(n)
 
     def c_copy(f, peer, place):
         return pltpu.make_async_remote_copy(
@@ -416,23 +417,7 @@
     for xx in range(CHIPS):
         scale(xx)
 
-    each_part(lambda peer: q_copy(peer, peer).wait_recv())
-    total = score_buf[0]
-    for i in range(1, 8):
-        total = total + score_buf[i]
-    score_out[...] = total
-
-    for f in range(2):
-        each_peer(lambda peer: c_copy(f, peer, peer).wait_recv())
-        tok_out[:, f * LANES : (f + 1) * LANES] = dot(send_t[...], in_r[f]).astype(BF16)
-
-    def sent(peer):
-        for ch in range(4):
-            x_copy(ch, peer, seq).wait_send()
-        for f in range(2):
-            c_copy(f, peer, seq).wait_send()
-
-    each_peer(sent)
+    each_peer(lambda peer: [x_copy(ch, peer, seq).wait_send() for ch in range(4)])
     each_part(lambda peer: q_copy(peer, ex).wait_send())
     for ch in range(4):
         for k in range(7):
@@ -442,6 +427,18 @@
     for f in range(2):
         for k in range(6):
             r_copy(f, k).wait_send()
+
+    each_part(lambda peer: q_copy(peer, peer).wait_recv())
+    total = score_buf[0]
+    for i in range(1, 8):
+        total = total + score_buf[i]
+    score_out[...] = total
+
+    for f in range(2):
+        each_peer(lambda peer: c_copy(f, peer, peer).wait_recv())
+        tok_out[:, f * LANES : (f + 1) * LANES] = dot(send_t[...], in_r[f]).astype(BF16)
+
+    each_peer(lambda peer: [c_copy(f, peer, seq).wait_send() for f in range(2)])
 
 
 def store_kernel(

time: 74.5 us -> 73.2 us (0.983)
  Pallas kernels: 73.6 us -> 72.3 us
    pallas_call x1, Pallas kernels: 68.8 us -> 67.5 us  [shards(): pl.pallas_call(layer_kernel, out_shape=tuple((pltpu.VMEM(*r) for r in fir...]
where the time goes in v5:
time: 73.2 us; the launch traced here: 73.1 us
  Pallas kernels  72.3 us (99%)
  between operations  0.8 us (1%)
    pallas_call x1, Pallas kernels, shards(): pl.pallas_call(layer_kernel, out_shape=tuple((pltpu.VMEM(*r) for r in fir...  67.5 us
    pallas_call x1, Pallas kernels, shards(): pl.pallas_call(store_kernel, out_shape=tuple((shape(*r) for r in results)...  4.79 us

profile of v5, /device:TPU:0, one launch (start us, length us, event | category | flops | bytes accessed | tf_op | source)
XLA Modules:
  0.0 73.1 jit_solution(3369727344313356896)
XLA Ops:
  0.6 67.5 %layer.1 = (bf16[512,256]{1,0:T(8,128)(2,1)S(1)}, f32[1,512]{1,0:T(1,128)S(1)}, bf16[2048,1024]{1,0:T(8,128)(2,1)S(1)}, bf16[2048,1024]{1,0:T(8,128)(2,1)S(1)}, ...) custom-call(bf16[512,256]{1,0:T(8,128)(2,1)} %tokens.1, bf16[512,256]{1,0:T(8,128)(2,1)} %grads_in.1, ...), custom_call_target="tpu_custom_call" | custom-call | tf_op jit(solution)/shard_map/layer/pallas_call | solution.py:480
  68.1 4.8 %store.1 = (bf16[512,256]{1,0:T(8,128)(2,1)}, f32[1,512]{1,0:T(1,128)}, bf16[2048,1024]{1,0:T(8,128)(2,1)}, bf16[2048,1024]{1,0:T(8,128)(2,1)}, bf16[1024,2048]{1,0:T(8,128)(2,1)}) custom-call(bf16[512,256]{1,0:T(8,128)(2,1)S(1)} %get-tuple-element.16.tok, f32[1,512]{1,0:T(1,128)S(1)} %get-tuple-element.17.score, ...), custom_call_target="tpu_custom_call" | custom-call | tf_op jit(solution)/shard_map/store/pallas_call | solution.py:539

commit v6 on v5

--- a/solution.py
+++ b/solution.py
@@ -211,6 +211,12 @@
 
     def scale(xx):
         scaled[xx] = (gain_col[:, 0:1] * full[1, xx].astype(F32)).astype(BF16)
+
+    def back_part(xx, cc):
+        for n in range(HID // WIDE):
+            cols = slice(n * WIDE, (n + 1) * WIDE)
+            feats = part_of(cc)
+            back_acc[:, cols] = back_acc[:, cols] + dot_t(full[1, xx, :, feats], down_v[xx, cols, feats])
 
     def back(xx, first):
         def body(n):
@@ -269,10 +275,10 @@
     flip_rows(left)
     flip_rows(right)
     relay_opp(3)
+    back_part(opp, c)
     flip_rows(opp)
-    hidden_t[...] = hidden[...].T
     g_wait_both(1, 6)
-    back(opp, False)
+    back_part(opp, oc)
 
     def finish(i, carry):
         rows = pl.ds(pl.multiple_of(i * 16, 16), 16)
@@ -350,7 +356,6 @@
     for_chip(2)
     add_sibling(2)
     send_direct(0, 1)
-    for_sibling(3)
 
     def score_rows(i, carry):
         rows = pl.ds(pl.multiple_of(i * 16, 16), 16)
@@ -370,9 +375,10 @@
     send_final(0)
     send_direct(1, 0)
     send_direct(1, 1)
+    for_sibling(3)
+    send_final(1)
     for_chip(3)
     lax.fori_loop(0, CAP // 16, score_rows, 0, unroll=2)
-    send_final(1)
     score_part = jnp.sum(back_acc[:, 0:128].T, axis=0, keepdims=True)
     score_buf[ex] = score_part
     each_part(lambda peer: q_copy(peer, ex).start())
@@ -414,6 +420,7 @@
     give_back(1)
     weight_rows(right)
     weight_rows(opp)
+    hidden_t[...] = hidden[...].T
     for xx in range(CHIPS):
         scale(xx)
 

time: 73.2 us -> 72.9 us (level)
  no operation moved by 1% of the time
where the time goes in v6:
time: 72.9 us; the launch traced here: 72.8 us
  Pallas kernels  72 us (99%)
  between operations  0.8 us (1%)
    pallas_call x1, Pallas kernels, shards(): pl.pallas_call(layer_kernel, out_shape=tuple((pltpu.VMEM(*r) for r in fir...  67.2 us
    pallas_call x1, Pallas kernels, shards(): pl.pallas_call(store_kernel, out_shape=tuple((shape(*r) for r in results)...  4.79 us

profile of v6, /device:TPU:0, one launch (start us, length us, event | category | flops | bytes accessed | tf_op | source)
XLA Modules:
  0.0 72.8 jit_solution(2384638547075576149)
XLA Ops:
  0.6 67.2 %layer.1 = (bf16[512,256]{1,0:T(8,128)(2,1)S(1)}, f32[1,512]{1,0:T(1,128)S(1)}, bf16[2048,1024]{1,0:T(8,128)(2,1)S(1)}, bf16[2048,1024]{1,0:T(8,128)(2,1)S(1)}, ...) custom-call(bf16[512,256]{1,0:T(8,128)(2,1)} %tokens.1, bf16[512,256]{1,0:T(8,128)(2,1)} %grads_in.1, ...), custom_call_target="tpu_custom_call" | custom-call | tf_op jit(solution)/shard_map/layer/pallas_call | solution.py:487
  67.8 4.8 %store.1 = (bf16[512,256]{1,0:T(8,128)(2,1)}, f32[1,512]{1,0:T(1,128)}, bf16[2048,1024]{1,0:T(8,128)(2,1)}, bf16[2048,1024]{1,0:T(8,128)(2,1)}, bf16[1024,2048]{1,0:T(8,128)(2,1)}) custom-call(bf16[512,256]{1,0:T(8,128)(2,1)S(1)} %get-tuple-element.16.tok, f32[1,512]{1,0:T(1,128)S(1)} %get-tuple-element.17.score, ...), custom_call_target="tpu_custom_call" | custom-call | tf_op jit(solution)/shard_map/store/pallas_call | solution.py:546
